TPU v7x, 512 devices: a whole 4x8x8 slice. The times are simulated.
512 devices in a mesh: dp: 4 (over x), tensor: 32 (over z_lo, y, core), section: 4 (over z_hi).
Axes of the slice: x: 4, y: 8, z: 8 (z_hi: 4, z_lo: 2; z = z_hi * 2 + z_lo), core: 2. Of those that a mesh axis runs over, the one named last changes fastest.
Arguments:
- partials: bfloat16 [32, 256, 16384], P('tensor', 'dp', 'section'), may hold values from -3 to 3
- residual: bfloat16 [256, 16384], P('dp', 'section'), may hold values from -300 to 300
- norm_gain: bfloat16 [16384], P('section'), may hold values from 0.5 to 1.5
- head_weight: bfloat16 [16384, 65536], P(('section', 'dp'), 'tensor'), may hold values from -0.234375 to 0.234375
- draft_logits: bfloat16 [4, 4, 32, 4, 8192], P('dp', 'section', 'tensor'), may hold values from -300 to 300
- draft_tokens: int32 [64, 4], P(('dp', 'section')), may hold values from 0 to 65535
- live_drafts: int32 [64], P(('dp', 'section')), may hold values from 1 to 4
Outputs:
- residual_rows: float32 [256, 65536], P(('dp', 'section'), 'tensor')
- accept_log: float32 [64, 4], P(('dp', 'section'))
All inputs are finite; a program needn't handle non-finite values.
Results may differ from a plain program's by a relative error of at most 0.0082.
Values may be sent and summed in bfloat16 or wider, within the bound.
No kernel may reach another device: no remote copies, remote signals or barrier semaphores. Data moves between devices by JAX's collectives and lax.ppermute only.
A program may use at most 64 MiB of HBM per device.

v0:
```python
import jax
import jax.numpy as jnp
from jax import lax
from jax.sharding import PartitionSpec as P

norm_epsilon = 1e-05


def partner(array, axis, stride):
    return lax.ppermute(array, axis, [(i, i ^ 1 << stride) for i in range(lax.axis_size(axis))])


def per_device(partials, residual, norm_gain, head_weight, draft_logits, draft_tokens, live_drafts):
    layer_term = partials[0].astype(jnp.float32)
    sections = lax.axis_size("section")
    owners = lax.axis_size("tensor")
    feature_count = layer_term.shape[1] * sections
    gain_row = norm_gain.astype(jnp.float32)
    layer_total = lax.psum(layer_term, "tensor")
    rounded = lax.optimization_barrier(
        (residual.astype(jnp.float32) + layer_total).astype(jnp.bfloat16)
    )
    hidden = rounded.astype(jnp.float32)
    squares = lax.psum(jnp.sum(hidden * hidden, axis=1), "section")
    factor = lax.rsqrt(squares / feature_count + norm_epsilon)
    normed = (hidden * factor[:, None] * gain_row).astype(jnp.bfloat16)
    head_in = lax.all_to_all(normed, "dp", split_axis=1, concat_axis=0, tiled=True)
    seq_count, draft_span = draft_tokens.shape
    row_count = seq_count * draft_span
    vocab_slice = head_weight.shape[1]
    everything = lax.psum(
        jnp.dot(head_in, head_weight, preferred_element_type=jnp.float32), ("dp", "section")
    )
    row_offset = (lax.axis_index("dp") * sections + lax.axis_index("section")) * row_count
    logits = lax.dynamic_slice_in_dim(everything, row_offset, row_count, 0)
    draft_block = draft_logits[0, 0, 0]
    group_size = owners // min(8, owners)
    my_slot = lax.axis_index("tensor") % group_size
    source_rows = draft_block.shape[0]
    pieces = jnp.transpose(draft_block.reshape(source_rows, group_size, vocab_slice), (1, 0, 2))
    for bit_level in range(group_size.bit_length() - 1):
        step_size = 1 << bit_level
        halves = pieces.reshape(
            group_size // (2 * step_size), 2, step_size, source_rows, vocab_slice
        )
        upper_bit = my_slot >> bit_level & 1 == 1
        kept_part = jnp.where(upper_bit, halves[:, 1], halves[:, 0])
        sent_part = jnp.where(upper_bit, halves[:, 0], halves[:, 1])
        received = partner(sent_part, "tensor", bit_level)
        lower_part = jnp.where(upper_bit, received, kept_part)
        upper_part = jnp.where(upper_bit, kept_part, received)
        pieces = jnp.stack([lower_part, upper_part], axis=1).reshape(
            group_size, source_rows, vocab_slice
        )
    drafted = pieces.reshape(row_count, vocab_slice).astype(jnp.float32)
    tokens_flat = draft_tokens.reshape(row_count)
    local_ids = tokens_flat - lax.axis_index("tensor") * vocab_slice
    chosen = lax.broadcasted_iota(jnp.int32, (row_count, vocab_slice), 1) == local_ids[:, None]
    picked_target = jnp.sum(jnp.where(chosen, logits, 0.0), axis=1)
    picked_draft = jnp.sum(jnp.where(chosen, drafted, 0.0), axis=1)
    peak_target, peak_draft = lax.pmax(
        (jnp.max(logits, axis=1), jnp.max(drafted, axis=1)), "tensor"
    )
    exp_target = jnp.exp(logits - peak_target[:, None])
    exp_draft = jnp.exp(drafted - peak_draft[:, None])
    total_target, total_draft, pick_target, pick_draft = lax.psum(
        (jnp.sum(exp_target, axis=1), jnp.sum(exp_draft, axis=1), picked_target, picked_draft),
        "tensor",
    )
    target_probs = exp_target / total_target[:, None]
    draft_probs = exp_draft / total_draft[:, None]
    excess = jnp.maximum(target_probs - draft_probs, 0.0)
    excess_mass = lax.psum(jnp.sum(excess, axis=1), "tensor")
    vocab_total = vocab_slice * owners
    position = lax.broadcasted_iota(jnp.int32, (row_count,), 0) % draft_span
    live_mask = position < jnp.repeat(live_drafts, draft_span)
    residual_rows = jnp.where(
        live_mask[:, None], vocab_total * excess / (excess_mass[:, None] + 1e-06), 0.0
    )
    log_ratio = (
        pick_target
        - peak_target
        - jnp.log(total_target)
        - (pick_draft - peak_draft - jnp.log(total_draft))
    )
    log_steps = jnp.where(live_mask, jnp.minimum(log_ratio, 0.0), 0.0).reshape(
        seq_count, draft_span
    )
    accept_log = jnp.where(
        live_mask.reshape(seq_count, draft_span), jnp.cumsum(log_steps, axis=1), 0.0
    )
    return (residual_rows, accept_log)


def solution(mesh):
    return jax.shard_map(
        per_device,
        mesh=mesh,
        in_specs=(
            P("tensor", "dp", "section"),
            P("dp", "section"),
            P("section"),
            P(("section", "dp"), "tensor"),
            P("dp", "section", "tensor", None, None),
            P(("dp", "section"), None),
            P(("dp", "section")),
        ),
        out_specs=(P(("dp", "section"), "tensor"), P(("dp", "section"), None)),
        check_vma=False,
    )
```

profile of v0, /device:TPU:1, one launch (start us, length us, event | category | flops | bytes accessed | tf_op | source)
XLA Modules:
  0.0 628.0 jit_solution(10442806714090219782)
XLA Ops:
  7.2 2.2 bitcast_convert_fusion
  9.5 236.0 %all-reduce.6.cloned.1.call-done = f32[64,4096]{1,0:T(8,128)} async-done(((f32[64,4096]{1,0:T(8,128)}), f32[64,4096]{1,0:T(8,128)}) %all-reduce.6.cloned.1.call-update) | async-done | bytes 1048592 | tf_op jit(solution)/shard_map/psum | solution.py:19
  245.5 1.3 add_convert_fusion
  246.8 0.2 fusion
  247.0 10.4 %psum.57 = f32[64]{0:T(128)S(1)} all-reduce(f32[64]{0:T(128)S(1)} %fusion), channel_id=1, replica_groups=mesh['dp'=4,'tensor'=32,'section'=4] {'section'}, use_global_device_ids=true, to_apply=%region_2.0 | all-reduce | flops 64 | bytes 512 | tf_op jit(solution)/shard_map/psum | solution.py:24
  257.4 0.2 fusion.2
  257.6 0.8 copy.43
  258.5 4.0 all-to-all-start
  262.5 5.2 collective-permute-start
  267.6 1.7 all-to-all-done
  269.4 4.7 fusion.15
  274.1 0.7 copy-done.4
  274.8 0.1 reshape.210
  275.1 1.9 collective-permute-start.1
  277.0 0.1 sub.74
  277.1 2.6 collective-permute-done.1
  279.8 0.1 fusion.13
  279.9 0.1 reshape.215
  280.0 166.6 %all-reduce.8.cloned.1.call-done = f32[256,2048]{1,0:T(8,128)} async-done(((f32[256,2048]{1,0:T(8,128)}), f32[256,2048]{1,0:T(8,128)}) %all-reduce.8.cloned.1.call-update) | async-done | bytes 2097168 | tf_op jit(solution)/shard_map/psum | solution.py:31
  446.6 1.0 dynamic-slice_reduce_fusion
  447.7 63.1 %all-reduce.2 = (f32[16]{0:T(128)S(1)}, f32[16]{0:T(128)S(1)}) all-reduce(f32[16]{0:T(128)S(1)} %reshape.215, f32[16]{0:T(128)S(1)} %dynamic-slice_reduce_fusion), channel_id=1, replica_groups=mesh['dp'=4,'tensor'=32,'section'=4] {'tensor'}, use_global_device_ids=true, to_apply=%region_9.10 | all-reduce | flops 32 | bytes 256 | tf_op jit(solution)/shard_map/pmax | solution.py:61
  510.8 0.1 sub.68
  510.9 0.2 select_reduce_fusion
  511.1 0.1 reduce_sum.61
  511.3 1.1 select_reduce_fusion.1
  512.4 53.0 %all-reduce.1 = (f32[16]{0:T(128)S(1)}, f32[16]{0:T(128)S(1)}) all-reduce(f32[16]{0:T(128)S(1)} %reduce_sum.61, f32[16]{0:T(128)S(1)} %get-tuple-element.3), channel_id=1, replica_groups=mesh['dp'=4,'tensor'=32,'section'=4] {'tensor'}, use_global_device_ids=true, to_apply=%region_11.12 | all-reduce | flops 32 | bytes 256 | tf_op jit(solution)/shard_map/psum | solution.py:66
  565.4 1.1 fusion.14
  566.5 53.0 %all-reduce = (f32[16]{0:T(128)S(1)}, f32[16]{0:T(128)S(1)}, f32[16]{0:T(128)S(1)}) all-reduce(f32[16]{0:T(128)S(1)} %get-tuple-element.13, f32[16]{0:T(128)S(1)} %reduce_sum.65, f32[16]{0:T(128)S(1)} %get-tuple-element.2), channel_id=1, replica_groups=mesh['dp'=4,'tensor'=32,'section'=4] {'tensor'}, use_global_device_ids=true, to_apply=%region_13.14 | all-reduce | flops 48 | bytes 384 | tf_op jit(solution)/shard_map/psum | solution.py:73
  619.5 0.1 reshape.212
  619.6 0.2 reduce_window_sum.11
  619.8 0.7 fusion.10
  620.4 0.7 divide_select_fusion
  (27 shorter events, 0.5 us)
Async XLA Ops:
  7.2 2.3 copy-start.2
  7.2 238.3 %copy-start = (bf16[64,4096]{1,0:T(8,128)(2,1)S(1)}, bf16[64,4096]{1,0:T(8,128)(2,1)}, u32[]{:S(2)}) copy-start(bf16[64,4096]{1,0:T(8,128)(2,1)} %param.8) | copy-start | bytes 1572868
  7.2 238.3 %all-reduce.6.cloned.1.call-start = ((), (), s32[]{:S(2)}) async-start(), calls=%async_computation.1 | async-start | bytes 2097152 | tf_op jit(solution)/shard_map/psum | solution.py:19
  246.8 15.6 %copy-start.1 = (bf16[1,1,1,4,8192]{4,3,2,1,0:T(4,128)(2,1)S(1)}, bf16[1,1,1,4,8192]{4,3,2,1,0:T(4,128)(2,1)}, u32[]{:S(2)}) copy-start(bf16[1,1,1,4,8192]{4,3,2,1,0:T(4,128)(2,1)} %param.11) | copy-start | bytes 196612
  258.5 10.9 %all-to-all-start = ((bf16[64,4,1024]{2,0,1:T(8,128)(2,1)}), bf16[64,4,1024]{2,0,1:T(8,128)(2,1)S(1)}, u32[]{:S(2)}, u32[]{:S(2)}) async-start(bf16[64,4,1024]{2,0,1:T(8,128)(2,1)} %bitcast.75), calls=%async_computation | async-start | bytes 1048576 | tf_op jit(solution)/shard_map/all_to_all | solution.py:27
  262.4 184.2 %all-reduce.8.cloned.1.call-start = ((), (), s32[]{:S(2)}) async-start(), calls=%async_computation.2 | async-start | bytes 4194304 | tf_op jit(solution)/shard_map/psum | solution.py:31
  262.5 12.5 %collective-permute-start = (bf16[2,1,4,2048]{3,2,0,1:T(4,128)(2,1)S(1)}, bf16[2,1,4,2048]{3,2,0,1:T(4,128)(2,1)S(1)}, u32[]{:S(2)}, u32[]{:S(2)}) collective-permute-start(bf16[2,1,4,2048]{3,2,0,1:T(4,128)(2,1)S(1)} %fusion.7), channel_id=1, source_target_pairs={{0,4},{4,0},{8,12},{12,8},{16,20},{20,16},{24,28},{28,24},{32,36},... | collective-permute-start | bytes 98312 | tf_op jit(solution)/shard_map/ppermute | solution.py:10
  274.1 0.7 copy-start.4
  274.1 0.7 copy-start.3
  275.1 4.7 collective-permute-start.1
Sparse Core Ops, SparseCore 0:
  10.9 234.4 all-reduce.5
  274.2 172.3 all-reduce.7
where the time goes:
time: 629 us; the launch traced here: 628 us
  waiting for transfers between devices  407 us (65%)
  blocking collectives  179 us (28%)
  between operations  14.2 us (2%)
  starting transfers between devices  11.1 us (2%)
  other arithmetic  9.39 us (1%)
    psum x1, waiting for transfers between devices, per_device(): layer_total = lax.psum(layer_term, 'tensor')  236 us
    psum x1, waiting for transfers between devices, per_device(): lax.psum(jnp.dot(head_in, head_weight, preferred_element_type=jnp.float32...  167 us
    pmax x1, blocking collectives, per_device(): lax.pmax((jnp.max(logits, axis=1), jnp.max(drafted, axis=1)), 'tensor')  63.1 us
    psum x1, blocking collectives, per_device(): excess_mass = lax.psum(jnp.sum(excess, axis=1), 'tensor')  53 us
    psum x1, blocking collectives, per_device(): lax.psum((jnp.sum(exp_target, axis=1), jnp.sum(exp_draft, axis=1), picked...  53 us
  transfers between devices with their start and end apart: 5, of which 4 were waited for; matrix products, arithmetic and copies ran while one was open for 1% of the time, Pallas kernels for 0%

commit v1 on v0

v1 whole, which is shorter than its diff:
```python
import jax
import jax.numpy as jnp
from jax import lax
from jax.sharding import PartitionSpec as P

norm_epsilon = 1e-05
f32 = jnp.float32
bf16 = jnp.bfloat16
f16 = jnp.float16


def exchange(blocks, axis):
    return lax.all_to_all(blocks, axis, split_axis=0, concat_axis=0, tiled=True)


def share(block, axis):
    copies = lax.axis_size(axis)
    return exchange(jnp.broadcast_to(block[None], (copies,) + block.shape), axis)


def per_device(partials, residual, norm_gain, head_weight, draft_logits, draft_tokens, live_drafts):
    dps = lax.axis_size("dp")
    sections = lax.axis_size("section")
    owners = lax.axis_size("tensor")
    tensor_at = lax.axis_index("tensor")
    rows, width = residual.shape
    feature_count = width * sections
    own_rows = rows // owners
    depth, vocab_slice = head_weight.shape
    seq_count, draft_span = draft_tokens.shape
    row_count = seq_count * draft_span

    draft_block = draft_logits[0, 0, 0]
    source_rows, draft_width = draft_block.shape
    group_size = draft_width // vocab_slice
    groups = [list(range(g, g + group_size)) for g in range(0, owners, group_size)]
    draft_pieces = jnp.transpose(
        draft_block.reshape(source_rows, group_size, vocab_slice), (1, 0, 2)
    )

    terms = exchange(partials[0].reshape(owners, own_rows, width), "tensor")
    layer_total = jnp.sum(terms.astype(f32), axis=0)
    own_residual = lax.dynamic_slice_in_dim(residual, tensor_at * own_rows, own_rows, 0)

    hidden_wide = lax.reduce_precision(own_residual.astype(f32) + layer_total, 8, 7)
    squares_own = jnp.sum(hidden_wide * hidden_wide, axis=1)
    squares_block = jnp.pad(squares_own[:, None], ((0, 8 - own_rows), (0, 127)))
    squares = jnp.sum(share(squares_block, "section").reshape(sections, 8, 128), axis=0)
    factor = lax.rsqrt(squares[:own_rows, :1] / feature_count + norm_epsilon)
    normed_own = (hidden_wide * factor * norm_gain.astype(f32)[None, :]).astype(bf16)

    by_block = jnp.transpose(normed_own.reshape(own_rows, dps, depth), (1, 0, 2))
    to_send = jnp.broadcast_to(by_block[:, None], (dps, owners, own_rows, depth))
    normed = exchange(to_send.reshape(dps * owners, own_rows, depth), ("dp", "tensor"))
    normed = normed.reshape(dps * rows, depth)
    products = jnp.dot(normed, head_weight, preferred_element_type=f32).astype(f16)

    gathered = exchange(products, ("dp", "section"))
    gathered = gathered.reshape(dps * sections, row_count, vocab_slice)
    logits = jnp.sum(gathered.astype(f32), axis=0)

    drafted = lax.all_to_all(
        draft_pieces, "tensor", 0, 0, axis_index_groups=groups, tiled=True
    ).reshape(row_count, vocab_slice).astype(f32)

    tokens_flat = draft_tokens.reshape(row_count)
    local_ids = tokens_flat - tensor_at * vocab_slice
    chosen = lax.broadcasted_iota(jnp.int32, (row_count, vocab_slice), 1) == local_ids[:, None]

    def statistics(values):
        peak = jnp.max(values, axis=1)
        exps = jnp.exp(values - peak[:, None])
        pick = jnp.sum(jnp.where(chosen, values, 0.0), axis=1)
        return exps, [peak, jnp.sum(exps, axis=1), pick]

    exp_draft, stats_draft = statistics(drafted)
    exp_target, stats_target = statistics(logits)
    stats = jnp.stack(stats_target + stats_draft + [stats_target[0]] * 2)
    stats = jnp.pad(stats, ((0, 0), (0, 128 - row_count)))
    stats = share(stats, "tensor").reshape(owners, 8, 128)[:, :, :row_count]

    def combine(peaks, totals, picks, own_peak):
        peak = jnp.max(peaks, axis=0)
        total = jnp.sum(totals * jnp.exp(peaks - peak[None]), axis=0)
        return peak, total, jnp.sum(picks, axis=0), jnp.exp(own_peak - peak) / total

    peak_target, total_target, pick_target, scale_target = combine(
        stats[:, 0], stats[:, 1], stats[:, 2], stats_target[0]
    )
    peak_draft, total_draft, pick_draft, scale_draft = combine(
        stats[:, 3], stats[:, 4], stats[:, 5], stats_draft[0]
    )
    excess = jnp.maximum(
        exp_target * scale_target[:, None] - exp_draft * scale_draft[:, None], 0.0
    )
    mass = jnp.pad(jnp.sum(excess, axis=1), (0, 128 - row_count))
    mass = share(jnp.broadcast_to(mass[None], (8, 128)), "tensor").reshape(owners, 8, 128)
    excess_mass = jnp.sum(mass[:, 0, :row_count], axis=0)

    vocab_total = vocab_slice * owners
    position = lax.broadcasted_iota(jnp.int32, (row_count,), 0) % draft_span
    live_mask = position < jnp.repeat(live_drafts, draft_span)
    row_scale = jnp.where(live_mask, vocab_total / (excess_mass + 1e-06), 0.0)
    residual_rows = excess * row_scale[:, None]
    log_ratio = (
        pick_target
        - peak_target
        - jnp.log(total_target)
        - (pick_draft - peak_draft - jnp.log(total_draft))
    )
    log_steps = jnp.where(live_mask, jnp.minimum(log_ratio, 0.0), 0.0).reshape(
        seq_count, draft_span
    )
    accept_log = jnp.where(
        live_mask.reshape(seq_count, draft_span), jnp.cumsum(log_steps, axis=1), 0.0
    )
    return (residual_rows, accept_log)


def solution(mesh):
    return jax.shard_map(
        per_device,
        mesh=mesh,
        in_specs=(
            P("tensor", "dp", "section"),
            P("dp", "section"),
            P("section"),
            P(("section", "dp"), "tensor"),
            P("dp", "section", "tensor", None, None),
            P(("dp", "section"), None),
            P(("dp", "section")),
        ),
        out_specs=(P(("dp", "section"), "tensor"), P(("dp", "section"), None)),
        check_vma=False,
    )
```

time: 629 us -> 153 us (0.24)
  waiting for transfers between devices: 407 us -> 68.9 us
  blocking collectives: 179 us -> 29.5 us
  starting transfers between devices: 11.1 us -> 36.5 us
  between operations: 14.2 us -> 0.8 us
    psum x2 -> x0, waiting for transfers between devices: 403 us -> none  [the longest x1 236 us: per_device(): layer_total = lax.psum(layer_term, 'tensor')]
    psum x3 -> x0, blocking collectives: 116 us -> none  [the longest x1 53 us: per_device(): excess_mass = lax.psum(jnp.sum(excess, axis=1), 'tensor')]
    all_to_all x1 -> x6, waiting for transfers between devices: 1.73 us -> 68.9 us  [the longest x5 68.9 us: exchange(): return lax.all_to_all(blocks, axis, split_axis=0, concat_axis=0, tiled=True)]
    pmax x1 -> x0, blocking collectives: 63.1 us -> none  [per_device(): lax.pmax((jnp.max(logits, axis=1), jnp.max(drafted, axis=1)), 'tensor')]
    all_to_all x1 -> x6, starting transfers between devices: 3.97 us -> 36.5 us  [the longest x5 33.2 us: exchange(): return lax.all_to_all(blocks, axis, split_axis=0, concat_axis=0, tiled=True)]
    all_to_all x0 -> x1, blocking collectives: none -> 29.5 us  [exchange(): return lax.all_to_all(blocks, axis, split_axis=0, concat_axis=0, tiled=True)]
    ppermute x2 -> x0, starting transfers between devices: 7.09 us -> none  [partner(): lax.ppermute(array, axis, [(i, i ^ 1 << stride) for i in range(lax.axis_s...]
  transfers between devices with their start and end apart: 5 -> 6, of which waited for: 4 -> 5; matrix products, arithmetic and copies ran while one was open for 1% -> 5% of each run, Pallas kernels for 0% -> 0%
where the time goes in v1:
time: 153 us
  waiting for transfers between devices  68.9 us (45%)
  starting transfers between devices  36.5 us (24%)
  blocking collectives  29.5 us (19%)
  other arithmetic  6.28 us (4%)
  local copies, waits for them, and re-layouts  6.07 us (4%)
  matrix products  4.47 us (3%)
    all_to_all x5, waiting for transfers between devices, exchange(): return lax.all_to_all(blocks, axis, split_axis=0, concat_axis=0, tiled=True)  68.9 us
    all_to_all x5, starting transfers between devices, exchange(): return lax.all_to_all(blocks, axis, split_axis=0, concat_axis=0, tiled=True)  33.2 us
    all_to_all x1, blocking collectives, exchange(): return lax.all_to_all(blocks, axis, split_axis=0, concat_axis=0, tiled=True)  29.5 us
    dot_general x1, matrix products, per_device(): jnp.dot(normed, head_weight, preferred_element_type=f32).astype(f16)  4.47 us
    all_to_all x1, starting transfers between devices, per_device(): lax.all_to_all(draft_pieces, 'tensor', 0, 0, axis_index_groups=groups, ti...  3.28 us
  transfers between devices with their start and end apart: 6, of which 5 were waited for; matrix products, arithmetic and copies ran while one was open for 5% of the time, Pallas kernels for 0%

profile of v1, /device:TPU:1, one launch (start us, length us, event | category | flops | bytes accessed | tf_op | source)
XLA Modules:
  0.0 152.6 jit_solution(8114802705320007197)
XLA Ops:
  0.6 2.2 %reshape_squeeze.6 = bf16[32,2,4096]{2,1,0:T(2,128)(2,1)} reshape(bf16[1,64,4096]{2,1,0:T(8,128)(2,1)} %param.7) | data formatting | bytes 1048576 | tf_op jit(solution)/shard_map/reshape;squeeze | solution.py:41
  2.8 10.6 %all-to-all-start = ((bf16[32,2,4096]{2,1,0:T(2,128)(2,1)}), bf16[32,2,4096]{2,1,0:T(2,128)(2,1)S(1)}, u32[]{:S(2)}, u32[]{:S(2)}) async-start(bf16[32,2,4096]{2,1,0:T(2,128)(2,1)} %reshape_squeeze.6), calls=%async_computation | async-start | bytes 1048576 | tf_op jit(solution)/shard_map/all_to_all | solution.py:13
  13.4 16.6 %all-to-all-done = bf16[32,2,4096]{2,1,0:T(2,128)(2,1)S(1)} async-done(((bf16[32,2,4096]{2,1,0:T(2,128)(2,1)}), bf16[32,2,4096]{2,1,0:T(2,128)(2,1)S(1)}, u32[]{:S(2)}, u32[]{:S(2)}) %all-to-all-start) | async-done | bytes 524320 | tf_op jit(solution)/shard_map/all_to_all | solution.py:13
  29.9 0.4 convert_reduce_fusion.1
  30.4 1.0 multiply_reduce_fusion
  31.5 0.6 broadcast_in_dim.25
  32.1 9.1 %all-to-all-start.1 = ((f32[4,8,128]{2,1,0:T(8,128)}), f32[4,8,128]{2,1,0:T(8,128)S(1)}, u32[]{:S(2)}, u32[]{:S(2)}) async-start(f32[4,8,128]{2,1,0:T(8,128)} %broadcast_in_dim.25), calls=%async_computation.1 | async-start | bytes 32768 | tf_op jit(solution)/shard_map/all_to_all | solution.py:13
  41.2 0.7 convert_element_type.37
  41.9 5.9 %all-to-all-done.1 = f32[4,8,128]{2,1,0:T(8,128)S(1)} async-done(((f32[4,8,128]{2,1,0:T(8,128)}), f32[4,8,128]{2,1,0:T(8,128)S(1)}, u32[]{:S(2)}, u32[]{:S(2)}) %all-to-all-start.1) | async-done | bytes 16416 | tf_op jit(solution)/shard_map/all_to_all | solution.py:13
  47.8 0.1 rsqrt_reduce_fusion
  48.0 0.9 multiply_convert_fusion
  48.9 0.3 broadcast_in_dim.27
  49.2 29.5 %all_to_all.39 = bf16[128,2,1024]{2,1,0:T(2,128)(2,1)S(1)} all-to-all(bf16[128,2,1024]{2,1,0:T(2,128)(2,1)S(1)} %bitcast.20), channel_id=1, replica_groups=mesh['dp'=4,'tensor'=32,'section'=4] {'dp','tensor'}, dimensions={0} | all-to-all | bytes 1048576 | tf_op jit(solution)/shard_map/all_to_all | solution.py:13
  78.7 3.3 %all-to-all-start.4 = ((bf16[4,4,2048]{2,1,0:T(4,128)(2,1)}), bf16[4,4,2048]{2,1,0:T(4,128)(2,1)S(1)}, u32[]{:S(2)}, u32[]{:S(2)}) async-start(bf16[4,4,2048]{2,1,0:T(4,128)(2,1)} %bitcast.8), calls=%async_computation.4 | async-start | bytes 131072 | tf_op jit(solution)/shard_map/all_to_all | solution.py:62
  82.0 0.2 reshape.152
  82.2 4.5 %convolution_convert_fusion = f16[256,2048]{1,0:T(8,128)(2,1)} fusion(bf16[256,1024]{1,0:T(8,128)(2,1)S(1)} %reshape.152, bf16[1024,2048]{1,0:T(8,128)(2,1)} %param.10), kind=kOutput, calls=%fused_computation | convolution fusion | flops 1074266112 | bytes 5767168 | tf_op jit(solution)/shard_map/dot_general | solution.py:56
  86.7 3.7 %all-to-all-start.3 = ((f16[16,16,2048]{2,1,0:T(8,128)(2,1)}), f16[16,16,2048]{2,1,0:T(8,128)(2,1)S(1)}, u32[]{:S(2)}, u32[]{:S(2)}) async-start(f16[16,16,2048]{2,1,0:T(8,128)(2,1)} %bitcast.3), calls=%async_computation.3 | async-start | bytes 2097152 | tf_op jit(solution)/shard_map/all_to_all | solution.py:13
  90.7 0.3 select_reduce_fusion
  91.1 29.5 %all-to-all-done.3 = f16[16,16,2048]{2,1,0:T(8,128)(2,1)S(1)} async-done(((f16[16,16,2048]{2,1,0:T(8,128)(2,1)}), f16[16,16,2048]{2,1,0:T(8,128)(2,1)S(1)}, u32[]{:S(2)}, u32[]{:S(2)}) %all-to-all-start.3) | async-done | bytes 1048608 | tf_op jit(solution)/shard_map/all_to_all | solution.py:13
  120.6 0.2 convert_reduce_fusion
  120.7 0.1 reduce_max.53
  120.9 0.2 select_reduce_fusion.1
  121.1 0.7 broadcast_in_dim.55
  121.8 4.7 %all-to-all-start.5 = ((f32[32,8,128]{2,1,0:T(8,128)}), f32[32,8,128]{2,1,0:T(8,128)S(1)}, u32[]{:S(2)}, u32[]{:S(2)}) async-start(f32[32,8,128]{2,1,0:T(8,128)} %broadcast_in_dim.55), calls=%async_computation.5 | async-start | bytes 262144 | tf_op jit(solution)/shard_map/all_to_all | solution.py:13
  126.9 8.7 %all-to-all-done.5 = f32[32,8,128]{2,1,0:T(8,128)S(1)} async-done(((f32[32,8,128]{2,1,0:T(8,128)}), f32[32,8,128]{2,1,0:T(8,128)S(1)}, u32[]{:S(2)}, u32[]{:S(2)}) %all-to-all-start.5) | async-done | bytes 131104 | tf_op jit(solution)/shard_map/all_to_all | solution.py:13
  136.4 0.3 maximum_reduce_fusion
  136.7 0.7 broadcast_in_dim_broadcast_in_dim_broadcast_in_dim.2
  137.4 5.1 %all-to-all-start.6 = ((f32[32,8,128]{2,1,0:T(8,128)}), f32[32,8,128]{2,1,0:T(8,128)S(1)}, u32[]{:S(2)}, u32[]{:S(2)}) async-start(f32[32,8,128]{2,1,0:T(8,128)} %broadcast_in_dim_broadcast_in_dim_broadcast_in_dim.2), calls=%async_computation.6 | async-start | bytes 262144 | tf_op jit(solution)/shard_map/all_to_all | solution.py:13
  142.6 0.2 reduce_window_sum.11
  142.8 0.7 broadcast_select_fusion
  143.4 8.3 %all-to-all-done.6 = f32[32,8,128]{2,1,0:T(8,128)S(1)} async-done(((f32[32,8,128]{2,1,0:T(8,128)}), f32[32,8,128]{2,1,0:T(8,128)S(1)}, u32[]{:S(2)}, u32[]{:S(2)}) %all-to-all-start.6) | async-done | bytes 131104 | tf_op jit(solution)/shard_map/all_to_all | solution.py:13
  151.8 0.8 maximum_multiply_fusion
  (42 shorter events, 2.0 us)
Async XLA Ops:
  2.8 27.1 %all-to-all-start = ((bf16[32,2,4096]{2,1,0:T(2,128)(2,1)}), bf16[32,2,4096]{2,1,0:T(2,128)(2,1)S(1)}, u32[]{:S(2)}, u32[]{:S(2)}) async-start(bf16[32,2,4096]{2,1,0:T(2,128)(2,1)} %reshape_squeeze.6), calls=%async_computation | async-start | bytes 1048576 | tf_op jit(solution)/shard_map/all_to_all | solution.py:13
  32.1 15.7 %all-to-all-start.1 = ((f32[4,8,128]{2,1,0:T(8,128)}), f32[4,8,128]{2,1,0:T(8,128)S(1)}, u32[]{:S(2)}, u32[]{:S(2)}) async-start(f32[4,8,128]{2,1,0:T(8,128)} %broadcast_in_dim.25), calls=%async_computation.1 | async-start | bytes 32768 | tf_op jit(solution)/shard_map/all_to_all | solution.py:13
  78.7 8.0 %all-to-all-start.4 = ((bf16[4,4,2048]{2,1,0:T(4,128)(2,1)}), bf16[4,4,2048]{2,1,0:T(4,128)(2,1)S(1)}, u32[]{:S(2)}, u32[]{:S(2)}) async-start(bf16[4,4,2048]{2,1,0:T(4,128)(2,1)} %bitcast.8), calls=%async_computation.4 | async-start | bytes 131072 | tf_op jit(solution)/shard_map/all_to_all | solution.py:62
  82.2 8.2 %copy-start.1 = (s32[4,4]{1,0:T(4,128)S(1)}, s32[4,4]{1,0:T(4,128)}, u32[]{:S(2)}) copy-start(s32[4,4]{1,0:T(4,128)} %param.12) | copy-start | bytes 196
  82.2 44.3 %copy-start = (s32[4]{0:T(128)S(1)}, s32[4]{0:T(128)}, u32[]{:S(2)}) copy-start(s32[4]{0:T(128)} %param.13) | copy-start | bytes 52
  86.7 33.9 %all-to-all-start.3 = ((f16[16,16,2048]{2,1,0:T(8,128)(2,1)}), f16[16,16,2048]{2,1,0:T(8,128)(2,1)S(1)}, u32[]{:S(2)}, u32[]{:S(2)}) async-start(f16[16,16,2048]{2,1,0:T(8,128)(2,1)} %bitcast.3), calls=%async_computation.3 | async-start | bytes 2097152 | tf_op jit(solution)/shard_map/all_to_all | solution.py:13
  121.8 13.8 %all-to-all-start.5 = ((f32[32,8,128]{2,1,0:T(8,128)}), f32[32,8,128]{2,1,0:T(8,128)S(1)}, u32[]{:S(2)}, u32[]{:S(2)}) async-start(f32[32,8,128]{2,1,0:T(8,128)} %broadcast_in_dim.55), calls=%async_computation.5 | async-start | bytes 262144 | tf_op jit(solution)/shard_map/all_to_all | solution.py:13
  137.4 14.3 %all-to-all-start.6 = ((f32[32,8,128]{2,1,0:T(8,128)}), f32[32,8,128]{2,1,0:T(8,128)S(1)}, u32[]{:S(2)}, u32[]{:S(2)}) async-start(f32[32,8,128]{2,1,0:T(8,128)} %broadcast_in_dim_broadcast_in_dim_broadcast_in_dim.2), calls=%async_computation.6 | async-start | bytes 262144 | tf_op jit(solution)/shard_map/all_to_all | solution.py:13

commit v2 on v1

v2 whole, which is shorter than its diff:
```python
import jax
import jax.numpy as jnp
from jax import lax
from jax.experimental import pallas as pl
from jax.experimental.pallas import tpu as pltpu
from jax.sharding import Mesh, PartitionSpec as P

norm_epsilon = 1e-05
f32 = jnp.float32
bf16 = jnp.bfloat16
f16 = jnp.float16
tensor_axes = ("zy", "core")


def exchange(blocks, axis):
    return lax.all_to_all(blocks, axis, split_axis=0, concat_axis=0, tiled=True)


def share(values):
    copies = lax.axis_size(tensor_axes)
    row = jnp.pad(values[None], ((0, 0), (0, 128 - values.shape[0])))
    return exchange(jnp.broadcast_to(row[None], (copies, 1, 128)), tensor_axes)


def head_kernel(x_ref, w_ref, o_ref):
    o_ref[...] = jnp.dot(x_ref[...], w_ref[...], preferred_element_type=f32)


def head_product(x, w):
    rows, depth = x.shape
    columns = w.shape[1]
    step = min(1024, columns)
    return pl.pallas_call(
        head_kernel,
        grid=(columns // step,),
        in_specs=[
            pl.BlockSpec((rows, depth), lambda i: (0, 0)),
            pl.BlockSpec((depth, step), lambda i: (0, i)),
        ],
        out_specs=pl.BlockSpec((rows, step), lambda i: (0, i)),
        out_shape=jax.ShapeDtypeStruct((rows, columns), f32),
        compiler_params=pltpu.CompilerParams(vmem_limit_bytes=16 << 20),
        name="head_product",
    )(x, w)


def per_device(partials, residual, norm_gain, head_weight, draft_logits, draft_tokens, live_drafts):
    dps = lax.axis_size("dp")
    sections = lax.axis_size("section")
    cores = lax.axis_size("core")
    owners = lax.axis_size(tensor_axes)
    chips = owners // cores
    tensor_at = lax.axis_index(tensor_axes)
    core_at = lax.axis_index("core")
    rows, width = residual.shape
    feature_count = width * sections
    own_rows = rows // owners
    depth, vocab_slice = head_weight.shape
    seq_count, draft_span = draft_tokens.shape
    row_count = seq_count * draft_span

    terms = exchange(partials[0].reshape(owners, own_rows, width), ("core", "zy"))
    layer_total = jnp.sum(terms.astype(f32), axis=0)
    own_at = (core_at * chips + lax.axis_index("zy")) * own_rows
    own_residual = lax.dynamic_slice_in_dim(residual, own_at, own_rows, 0)

    hidden = lax.reduce_precision(own_residual.astype(f32) + layer_total, 8, 7)
    squares = lax.psum(jnp.sum(hidden * hidden, axis=1), "section")
    factor = lax.rsqrt(squares / feature_count + norm_epsilon)
    normed_own = (hidden * factor[:, None] * norm_gain.astype(f32)[None, :]).astype(bf16)

    by_block = jnp.transpose(normed_own.reshape(own_rows, dps, depth), (1, 0, 2))
    to_send = jnp.broadcast_to(by_block[:, None], (dps, chips, own_rows, depth))
    mine = exchange(to_send.reshape(dps * chips, own_rows, depth), ("dp", "zy"))
    mine = mine.reshape(dps, rows // cores, depth)
    other = lax.ppermute(mine, "core", [(0, 1), (1, 0)])
    normed = jnp.where(
        core_at == 0, jnp.stack([mine, other], axis=1), jnp.stack([other, mine], axis=1)
    ).reshape(dps * rows, depth)
    products = head_product(normed, head_weight).astype(f16)

    by_dp = exchange(products, "dp").reshape(dps, rows, vocab_slice)
    by_dp = jnp.sum(by_dp.astype(f32), axis=0).astype(f16)
    gathered = exchange(by_dp, "section").reshape(sections, row_count, vocab_slice)
    logits = jnp.sum(gathered.astype(f32), axis=0)

    draft_block = draft_logits[0, 0, 0]
    source_rows, draft_width = draft_block.shape
    group_size = draft_width // vocab_slice
    member = tensor_at % group_size
    pieces = jnp.transpose(
        draft_block.reshape(source_rows, group_size, vocab_slice), (1, 0, 2)
    )
    arrived = []
    for flip in range(group_size):
        piece = lax.dynamic_index_in_dim(pieces, member ^ flip, 0, keepdims=False)
        if flip:
            piece = lax.ppermute(piece, tensor_axes, [(i, i ^ flip) for i in range(owners)])
        arrived.append(piece)
    arrived = jnp.stack(arrived)
    drafted = jnp.concatenate(
        [
            lax.dynamic_index_in_dim(arrived, member ^ source, 0, keepdims=False)
            for source in range(group_size)
        ]
    ).astype(f32)

    tokens_flat = draft_tokens.reshape(row_count)
    local_ids = tokens_flat - tensor_at * vocab_slice
    chosen = lax.broadcasted_iota(jnp.int32, (row_count, vocab_slice), 1) == local_ids[:, None]

    def statistics(values):
        peak = jnp.max(values, axis=1)
        exps = jnp.exp(values - peak[:, None])
        pick = jnp.sum(jnp.where(chosen, values, 0.0), axis=1)
        return exps, [peak, jnp.sum(exps, axis=1), pick]

    exp_draft, stats_draft = statistics(drafted)
    exp_target, stats_target = statistics(logits)
    stats = share(jnp.concatenate(stats_target + stats_draft))
    stats = stats[:, 0, : 6 * row_count].reshape(owners, 6, row_count)

    def combine(peaks, totals, picks, own_peak):
        peak = jnp.max(peaks, axis=0)
        total = jnp.sum(totals * jnp.exp(peaks - peak[None]), axis=0)
        return peak, total, jnp.sum(picks, axis=0), jnp.exp(own_peak - peak) / total

    peak_target, total_target, pick_target, scale_target = combine(
        stats[:, 0], stats[:, 1], stats[:, 2], stats_target[0]
    )
    peak_draft, total_draft, pick_draft, scale_draft = combine(
        stats[:, 3], stats[:, 4], stats[:, 5], stats_draft[0]
    )
    excess = jnp.maximum(
        exp_target * scale_target[:, None] - exp_draft * scale_draft[:, None], 0.0
    )
    mass = share(jnp.sum(excess, axis=1))
    excess_mass = jnp.sum(mass[:, 0, :row_count], axis=0)

    vocab_total = vocab_slice * owners
    position = lax.broadcasted_iota(jnp.int32, (row_count,), 0) % draft_span
    live_mask = position < jnp.repeat(live_drafts, draft_span)
    row_scale = jnp.where(live_mask, vocab_total / (excess_mass + 1e-06), 0.0)
    residual_rows = excess * row_scale[:, None]
    log_ratio = (
        pick_target
        - peak_target
        - jnp.log(total_target)
        - (pick_draft - peak_draft - jnp.log(total_draft))
    )
    log_steps = jnp.where(live_mask, jnp.minimum(log_ratio, 0.0), 0.0).reshape(
        seq_count, draft_span
    )
    accept_log = jnp.where(
        live_mask.reshape(seq_count, draft_span), jnp.cumsum(log_steps, axis=1), 0.0
    )
    return (residual_rows, accept_log)


def solution(mesh):
    sizes = mesh.shape
    split = Mesh(
        mesh.devices.reshape(sizes["dp"], sizes["tensor"] // 2, 2, sizes["section"]),
        ("dp",) + tensor_axes + ("section",),
    )
    return jax.shard_map(
        per_device,
        mesh=split,
        in_specs=(
            P(tensor_axes, "dp", "section"),
            P("dp", "section"),
            P("section"),
            P(("section", "dp"), tensor_axes),
            P("dp", "section", tensor_axes, None, None),
            P(("dp", "section"), None),
            P(("dp", "section")),
        ),
        out_specs=(P(("dp", "section"), tensor_axes), P(("dp", "section"), None)),
        check_vma=False,
    )
```

time: 153 us -> 139 us (0.908)
  waiting for transfers between devices: 68.9 us -> 45.8 us
  starting transfers between devices: 36.5 us -> 42.3 us
  matrix products: 4.47 us -> 0 us
  blocking collectives: 29.5 us -> 33.7 us
  Pallas kernels: 0 us -> 1.84 us
    all_to_all x5, waiting for transfers between devices: 68.9 us -> 44.7 us  [exchange(): return lax.all_to_all(blocks, axis, split_axis=0, concat_axis=0, tiled=True)]
    psum x0 -> x1, blocking collectives: none -> 14.7 us  [per_device(): squares = lax.psum(jnp.sum(hidden * hidden, axis=1), 'section')]
    ppermute x0 -> x4, starting transfers between devices: none -> 13.8 us  [the longest x3 7.88 us: per_device(): lax.ppermute(piece, tensor_axes, [(i, i ^ flip) for i in range(owners)])]
    all_to_all x1, blocking collectives: 29.5 us -> 19 us  [exchange(): return lax.all_to_all(blocks, axis, split_axis=0, concat_axis=0, tiled=True)]
    all_to_all x5, starting transfers between devices: 33.2 us -> 28.5 us  [exchange(): return lax.all_to_all(blocks, axis, split_axis=0, concat_axis=0, tiled=True)]
    dot_general x1 -> x0, matrix products: 4.47 us -> none  [per_device(): jnp.dot(normed, head_weight, preferred_element_type=f32).astype(f16)]
    all_to_all x1 -> x0, starting transfers between devices: 3.28 us -> none  [per_device(): lax.all_to_all(draft_pieces, 'tensor', 0, 0, axis_index_groups=groups, ti...]
    unnamed x5 -> x11, local copies, waits for them, and re-layouts: 0.11 us -> 2.29 us
  transfers between devices with their start and end apart: 6 -> 9, of which waited for: 5 -> 6; matrix products, arithmetic and copies ran while one was open for 5% -> 2% of each run, Pallas kernels for 0% -> 0%
where the time goes in v2:
time: 139 us
  waiting for transfers between devices  45.8 us (33%)
  starting transfers between devices  42.3 us (30%)
  blocking collectives  33.7 us (24%)
  other arithmetic  7.45 us (5%)
  local copies, waits for them, and re-layouts  6.57 us (5%)
  Pallas kernels  1.84 us (1%)
    all_to_all x5, waiting for transfers between devices, exchange(): return lax.all_to_all(blocks, axis, split_axis=0, concat_axis=0, tiled=True)  44.7 us
    all_to_all x5, starting transfers between devices, exchange(): return lax.all_to_all(blocks, axis, split_axis=0, concat_axis=0, tiled=True)  28.5 us
    all_to_all x1, blocking collectives, exchange(): return lax.all_to_all(blocks, axis, split_axis=0, concat_axis=0, tiled=True)  19 us
    psum x1, blocking collectives, per_device(): squares = lax.psum(jnp.sum(hidden * hidden, axis=1), 'section')  14.7 us
    ppermute x3, starting transfers between devices, per_device(): lax.ppermute(piece, tensor_axes, [(i, i ^ flip) for i in range(owners)])  7.88 us
    ppermute x1, starting transfers between devices, per_device(): other = lax.ppermute(mine, 'core', [(0, 1), (1, 0)])  5.92 us
  transfers between devices with their start and end apart: 9, of which 6 were waited for; matrix products, arithmetic and copies ran while one was open for 2% of the time, Pallas kernels for 0%

profile of v2, /device:TPU:1, one launch (start us, length us, event | category | flops | bytes accessed | tf_op | source)
XLA Modules:
  0.0 138.6 jit_solution(2784608526413125368)
XLA Ops:
  0.6 2.2 %reshape_squeeze.9 = bf16[32,2,4096]{2,1,0:T(2,128)(2,1)} reshape(bf16[1,64,4096]{2,1,0:T(8,128)(2,1)} %param.7) | data formatting | bytes 1048576 | tf_op jit(solution)/shard_map/reshape;squeeze | solution.py:62
  2.8 10.6 %all-to-all-start = ((bf16[32,2,4096]{2,1,0:T(2,128)(2,1)}), bf16[32,2,4096]{2,1,0:T(2,128)(2,1)S(1)}, u32[]{:S(2)}, u32[]{:S(2)}) async-start(bf16[32,2,4096]{2,1,0:T(2,128)(2,1)} %reshape_squeeze.9), calls=%async_computation | async-start | bytes 1048576 | tf_op jit(solution)/shard_map/all_to_all | solution.py:16
  13.4 15.6 %all-to-all-done = bf16[32,2,4096]{2,1,0:T(2,128)(2,1)S(1)} async-done(((bf16[32,2,4096]{2,1,0:T(2,128)(2,1)}), bf16[32,2,4096]{2,1,0:T(2,128)(2,1)S(1)}, u32[]{:S(2)}, u32[]{:S(2)}) %all-to-all-start) | async-done | bytes 524320 | tf_op jit(solution)/shard_map/all_to_all | solution.py:16
  29.0 0.4 convert_reduce_fusion.1
  29.4 1.0 multiply_reduce_fusion
  30.4 14.7 %psum.7 = f32[2]{0:T(128)S(1)} all-reduce(f32[2]{0:T(128)S(1)} %multiply_reduce_fusion), channel_id=1, replica_groups=mesh['dp'=4,'zy'=16,'core'=2,'section'=4] {'section'}, use_global_device_ids=true, to_apply=%region_2.0 | all-reduce | flops 2 | bytes 16 | tf_op jit(solution)/shard_map/psum | solution.py:68
  45.2 0.9 multiply_convert_fusion
  46.3 19.0 %all_to_all.35 = bf16[64,2,1024]{2,1,0:T(2,128)(2,1)S(1)} all-to-all(bf16[64,2,1024]{2,1,0:T(2,128)(2,1)S(1)} %bitcast.59), channel_id=1, replica_groups=mesh['dp'=4,'zy'=16,'core'=2,'section'=4] {'dp','zy'}, dimensions={0} | all-to-all | bytes 524288 | tf_op jit(solution)/shard_map/all_to_all | solution.py:16
  65.4 5.9 %collective-permute-start = (bf16[4,32,1024]{2,1,0:T(8,128)(2,1)S(1)}, bf16[4,32,1024]{2,1,0:T(8,128)(2,1)S(1)}, u32[]{:S(2)}, u32[]{:S(2)}) collective-permute-start(bf16[4,32,1024]{2,1,0:T(8,128)(2,1)S(1)} %reshape.119), channel_id=1, source_target_pairs={{0,4},{4,0},{1,5},{5,1},{2,6},{6,2},{3,7},{7,3},{8,12},{12,8},{9,1... | collective-permute-start | bytes 786440 | tf_op jit(solution)/shard_map/ppermute | solution.py:76
  71.4 1.0 collective-permute-done
  72.5 2.2 %copy-done = bf16[1024,2048]{1,0:T(8,128)(2,1)S(1)} copy-done((bf16[1024,2048]{1,0:T(8,128)(2,1)S(1)}, bf16[1024,2048]{1,0:T(8,128)(2,1)}, u32[]{:S(2)}) %copy-start) | copy-done | bytes 4194328
  74.7 1.8 %head_product.1 = f32[256,2048]{1,0:T(8,128)S(1)} custom-call(bf16[256,1024]{1,0:T(8,128)(2,1)S(1)} %bitcast.58, bf16[1024,2048]{1,0:T(8,128)(2,1)S(1)} %copy-done), custom_call_target="tpu_custom_call" | custom-call | tf_op jit(solution)/shard_map/head_product/pallas_call | solution.py:33
  76.6 1.1 convert_element_type.39
  77.7 3.5 %all-to-all-start.2 = ((f16[4,64,2048]{2,1,0:T(8,128)(2,1)}), f16[4,64,2048]{2,1,0:T(8,128)(2,1)S(1)}, u32[]{:S(2)}, u32[]{:S(2)}) async-start(f16[4,64,2048]{2,1,0:T(8,128)(2,1)} %bitcast.4), calls=%async_computation.2 | async-start | bytes 2097152 | tf_op jit(solution)/shard_map/all_to_all | solution.py:16
  81.3 2.9 %collective-permute-start.3 = (bf16[4,2048]{1,0:T(4,128)(2,1)S(1)}, bf16[4,2048]{1,0:T(4,128)(2,1)S(1)}, u32[]{:S(2)}, u32[]{:S(2)}) collective-permute-start(bf16[4,2048]{1,0:T(4,128)(2,1)S(1)} %get-tuple-element.21), channel_id=1, source_target_pairs={{0,12},{4,8},{8,4},{12,0},{16,28},{20,24},{24,20},{28,16},{32,44},... | collective-permute-start | bytes 49160 | tf_op jit(solution)/shard_map/ppermute | solution.py:98
  84.3 2.6 %collective-permute-start.2 = (bf16[4,2048]{1,0:T(4,128)(2,1)S(1)}, bf16[4,2048]{1,0:T(4,128)(2,1)S(1)}, u32[]{:S(2)}, u32[]{:S(2)}) collective-permute-start(bf16[4,2048]{1,0:T(4,128)(2,1)S(1)} %get-tuple-element.22), channel_id=1, source_target_pairs={{0,8},{4,12},{8,0},{12,4},{16,24},{20,28},{24,16},{28,20},{32,40},... | collective-permute-start | bytes 49160 | tf_op jit(solution)/shard_map/ppermute | solution.py:98
  86.9 2.3 %collective-permute-start.1 = (bf16[4,2048]{1,0:T(4,128)(2,1)S(1)}, bf16[4,2048]{1,0:T(4,128)(2,1)S(1)}, u32[]{:S(2)}, u32[]{:S(2)}) collective-permute-start(bf16[4,2048]{1,0:T(4,128)(2,1)S(1)} %get-tuple-element.23), channel_id=1, source_target_pairs={{0,4},{4,0},{8,12},{12,8},{16,20},{20,16},{24,28},{28,24},{32,36},... | collective-permute-start | bytes 49160 | tf_op jit(solution)/shard_map/ppermute | solution.py:98
  89.4 6.7 %all-to-all-done.2 = f16[4,64,2048]{2,1,0:T(8,128)(2,1)S(1)} async-done(((f16[4,64,2048]{2,1,0:T(8,128)(2,1)}), f16[4,64,2048]{2,1,0:T(8,128)(2,1)S(1)}, u32[]{:S(2)}, u32[]{:S(2)}) %all-to-all-start.2) | async-done | bytes 1048608 | tf_op jit(solution)/shard_map/all_to_all | solution.py:16
  96.1 0.2 convert_reduce_fusion
  96.3 0.7 convert_element_type.41
  97.0 3.4 %all-to-all-start.3 = ((f16[4,16,2048]{2,1,0:T(8,128)(2,1)}), f16[4,16,2048]{2,1,0:T(8,128)(2,1)S(1)}, u32[]{:S(2)}, u32[]{:S(2)}) async-start(f16[4,16,2048]{2,1,0:T(8,128)(2,1)} %bitcast.5), calls=%async_computation.3 | async-start | bytes 524288 | tf_op jit(solution)/shard_map/all_to_all | solution.py:16
  100.7 7.9 %all-to-all-done.3 = f16[4,16,2048]{2,1,0:T(8,128)(2,1)S(1)} async-done(((f16[4,16,2048]{2,1,0:T(8,128)(2,1)}), f16[4,16,2048]{2,1,0:T(8,128)(2,1)S(1)}, u32[]{:S(2)}, u32[]{:S(2)}) %all-to-all-start.3) | async-done | bytes 262176 | tf_op jit(solution)/shard_map/all_to_all | solution.py:16
  108.8 0.3 fusion.5
  109.1 0.6 broadcast_in_dim.59
  109.7 6.7 %all-to-all-start.4 = ((f32[32,1,128]{2,1,0:T(1,128)}), f32[32,1,128]{2,1,0:T(1,128)S(1)}, u32[]{:S(2)}, u32[]{:S(2)}) async-start(f32[32,1,128]{2,1,0:T(1,128)} %broadcast_in_dim.59), calls=%async_computation.4 | async-start | bytes 32768 | tf_op jit(solution)/shard_map/all_to_all | solution.py:16
  116.6 7.7 %all-to-all-done.4 = f32[32,1,128]{2,1,0:T(1,128)S(1)} async-done(((f32[32,1,128]{2,1,0:T(1,128)}), f32[32,1,128]{2,1,0:T(1,128)S(1)}, u32[]{:S(2)}, u32[]{:S(2)}) %all-to-all-start.4) | async-done | bytes 16416 | tf_op jit(solution)/shard_map/all_to_all | solution.py:16
  124.8 0.2 fusion.16
  125.0 0.6 broadcast_in_dim.63
  125.6 4.3 %all-to-all-start.5 = ((f32[32,1,128]{2,1,0:T(1,128)}), f32[32,1,128]{2,1,0:T(1,128)S(1)}, u32[]{:S(2)}, u32[]{:S(2)}) async-start(f32[32,1,128]{2,1,0:T(1,128)} %broadcast_in_dim.63), calls=%async_computation.5 | async-start | bytes 32768 | tf_op jit(solution)/shard_map/all_to_all | solution.py:16
  130.3 0.7 broadcast_select_fusion
  130.9 6.9 %all-to-all-done.5 = f32[32,1,128]{2,1,0:T(1,128)S(1)} async-done(((f32[32,1,128]{2,1,0:T(1,128)}), f32[32,1,128]{2,1,0:T(1,128)S(1)}, u32[]{:S(2)}, u32[]{:S(2)}) %all-to-all-start.5) | async-done | bytes 16416 | tf_op jit(solution)/shard_map/all_to_all | solution.py:16
  137.9 0.7 broadcast_multiply_fusion
  (43 shorter events, 2.1 us)
Async XLA Ops:
  0.6 29.8 %copy-start.2 = (bf16[4096]{0:T(1024)(128)(2,1)S(1)}, bf16[4096]{0:T(1024)(128)(2,1)}, u32[]{:S(2)}) copy-start(bf16[4096]{0:T(1024)(128)(2,1)} %param.9) | copy-start | bytes 24580
  2.8 26.2 %all-to-all-start = ((bf16[32,2,4096]{2,1,0:T(2,128)(2,1)}), bf16[32,2,4096]{2,1,0:T(2,128)(2,1)S(1)}, u32[]{:S(2)}, u32[]{:S(2)}) async-start(bf16[32,2,4096]{2,1,0:T(2,128)(2,1)} %reshape_squeeze.9), calls=%async_computation | async-start | bytes 1048576 | tf_op jit(solution)/shard_map/all_to_all | solution.py:16
  65.4 7.1 %collective-permute-start = (bf16[4,32,1024]{2,1,0:T(8,128)(2,1)S(1)}, bf16[4,32,1024]{2,1,0:T(8,128)(2,1)S(1)}, u32[]{:S(2)}, u32[]{:S(2)}) collective-permute-start(bf16[4,32,1024]{2,1,0:T(8,128)(2,1)S(1)} %reshape.119), channel_id=1, source_target_pairs={{0,4},{4,0},{1,5},{5,1},{2,6},{6,2},{3,7},{7,3},{8,12},{12,8},{9,1... | collective-permute-start | bytes 786440 | tf_op jit(solution)/shard_map/ppermute | solution.py:76
  72.5 2.2 %copy-start = (bf16[1024,2048]{1,0:T(8,128)(2,1)S(1)}, bf16[1024,2048]{1,0:T(8,128)(2,1)}, u32[]{:S(2)}) copy-start(bf16[1024,2048]{1,0:T(8,128)(2,1)} %w_ref.1) | copy-start | bytes 12582916
  76.5 4.7 %copy-start.1 = (bf16[1,1,1,4,8192]{4,3,2,1,0:T(4,128)(2,1)S(1)}, bf16[1,1,1,4,8192]{4,3,2,1,0:T(4,128)(2,1)}, u32[]{:S(2)}) copy-start(bf16[1,1,1,4,8192]{4,3,2,1,0:T(4,128)(2,1)} %param.11) | copy-start | bytes 196612
  76.6 12.7 %copy-start.4 = (s32[4,4]{1,0:T(4,128)S(1)}, s32[4,4]{1,0:T(4,128)}, u32[]{:S(2)}) copy-start(s32[4,4]{1,0:T(4,128)} %param.12) | copy-start | bytes 196
  77.7 18.3 %all-to-all-start.2 = ((f16[4,64,2048]{2,1,0:T(8,128)(2,1)}), f16[4,64,2048]{2,1,0:T(8,128)(2,1)S(1)}, u32[]{:S(2)}, u32[]{:S(2)}) async-start(f16[4,64,2048]{2,1,0:T(8,128)(2,1)} %bitcast.4), calls=%async_computation.2 | async-start | bytes 2097152 | tf_op jit(solution)/shard_map/all_to_all | solution.py:16
  81.3 35.2 %copy-start.3 = (s32[4]{0:T(128)S(1)}, s32[4]{0:T(128)}, u32[]{:S(2)}) copy-start(s32[4]{0:T(128)} %param.13) | copy-start | bytes 52
  81.3 19.1 %collective-permute-start.3 = (bf16[4,2048]{1,0:T(4,128)(2,1)S(1)}, bf16[4,2048]{1,0:T(4,128)(2,1)S(1)}, u32[]{:S(2)}, u32[]{:S(2)}) collective-permute-start(bf16[4,2048]{1,0:T(4,128)(2,1)S(1)} %get-tuple-element.21), channel_id=1, source_target_pairs={{0,12},{4,8},{8,4},{12,0},{16,28},{20,24},{24,20},{28,16},{32,44},... | collective-permute-start | bytes 49160 | tf_op jit(solution)/shard_map/ppermute | solution.py:98
  84.3 16.1 %collective-permute-start.2 = (bf16[4,2048]{1,0:T(4,128)(2,1)S(1)}, bf16[4,2048]{1,0:T(4,128)(2,1)S(1)}, u32[]{:S(2)}, u32[]{:S(2)}) collective-permute-start(bf16[4,2048]{1,0:T(4,128)(2,1)S(1)} %get-tuple-element.22), channel_id=1, source_target_pairs={{0,8},{4,12},{8,0},{12,4},{16,24},{20,28},{24,16},{28,20},{32,40},... | collective-permute-start | bytes 49160 | tf_op jit(solution)/shard_map/ppermute | solution.py:98
  86.9 13.5 %collective-permute-start.1 = (bf16[4,2048]{1,0:T(4,128)(2,1)S(1)}, bf16[4,2048]{1,0:T(4,128)(2,1)S(1)}, u32[]{:S(2)}, u32[]{:S(2)}) collective-permute-start(bf16[4,2048]{1,0:T(4,128)(2,1)S(1)} %get-tuple-element.23), channel_id=1, source_target_pairs={{0,4},{4,0},{8,12},{12,8},{16,20},{20,16},{24,28},{28,24},{32,36},... | collective-permute-start | bytes 49160 | tf_op jit(solution)/shard_map/ppermute | solution.py:98
  97.0 11.6 %all-to-all-start.3 = ((f16[4,16,2048]{2,1,0:T(8,128)(2,1)}), f16[4,16,2048]{2,1,0:T(8,128)(2,1)S(1)}, u32[]{:S(2)}, u32[]{:S(2)}) async-start(f16[4,16,2048]{2,1,0:T(8,128)(2,1)} %bitcast.5), calls=%async_computation.3 | async-start | bytes 524288 | tf_op jit(solution)/shard_map/all_to_all | solution.py:16
  109.7 14.6 %all-to-all-start.4 = ((f32[32,1,128]{2,1,0:T(1,128)}), f32[32,1,128]{2,1,0:T(1,128)S(1)}, u32[]{:S(2)}, u32[]{:S(2)}) async-start(f32[32,1,128]{2,1,0:T(1,128)} %broadcast_in_dim.59), calls=%async_computation.4 | async-start | bytes 32768 | tf_op jit(solution)/shard_map/all_to_all | solution.py:16
  125.6 12.2 %all-to-all-start.5 = ((f32[32,1,128]{2,1,0:T(1,128)}), f32[32,1,128]{2,1,0:T(1,128)S(1)}, u32[]{:S(2)}, u32[]{:S(2)}) async-start(f32[32,1,128]{2,1,0:T(1,128)} %broadcast_in_dim.63), calls=%async_computation.5 | async-start | bytes 32768 | tf_op jit(solution)/shard_map/all_to_all | solution.py:16

commit v3 on v2

v3 whole, which is shorter than its diff:
```python
import functools

import jax
import jax.numpy as jnp
from jax import lax
from jax.experimental import pallas as pl
from jax.experimental.pallas import tpu as pltpu
from jax.sharding import Mesh, PartitionSpec as P

norm_epsilon = 1e-05
f32 = jnp.float32
bf16 = jnp.bfloat16
f16 = jnp.float16
tensor_axes = ("zy", "core")


def exchange(blocks, axis):
    return lax.all_to_all(blocks, axis, split_axis=0, concat_axis=0, tiled=True)


def one_row(values):
    return jnp.pad(values[None], ((0, 0), (0, 128 - values.shape[0])))


def share(values):
    copies = lax.axis_size(tensor_axes)
    return exchange(jnp.broadcast_to(one_row(values)[None], (copies, 1, 128)), tensor_axes)


def head_kernel(x_ref, top_ref, w_hbm, o_ref, bottom, arrived):
    depth = top_ref.shape[0]
    part = depth // 2
    copies = [
        pltpu.make_async_copy(
            w_hbm.at[pl.ds(depth + i * part, part), :],
            bottom.at[pl.ds(i * part, part), :],
            arrived.at[i],
        )
        for i in range(2)
    ]
    for copy in copies:
        copy.start()
    o_ref[...] = jnp.dot(x_ref[:, :depth], top_ref[...], preferred_element_type=f32)
    for i, copy in enumerate(copies):
        copy.wait()
        o_ref[...] += jnp.dot(
            x_ref[:, depth + i * part : depth + (i + 1) * part],
            bottom[pl.ds(i * part, part), :],
            preferred_element_type=f32,
        )


def head_product(x, top, w):
    rows, columns = x.shape[0], w.shape[1]
    return pl.pallas_call(
        head_kernel,
        in_specs=[
            pl.BlockSpec(memory_space=pltpu.VMEM),
            pl.BlockSpec(memory_space=pltpu.VMEM),
            pl.BlockSpec(memory_space=pl.ANY),
        ],
        out_specs=pl.BlockSpec(memory_space=pltpu.VMEM),
        out_shape=jax.ShapeDtypeStruct((rows, columns), f32),
        scratch_shapes=[pltpu.VMEM(top.shape, w.dtype), pltpu.SemaphoreType.DMA((2,))],
        compiler_params=pltpu.CompilerParams(vmem_limit_bytes=48 << 20),
        name="head_product",
    )(x, top, w)


def finish_kernel(vocab_total, excess_ref, mass_ref, ratio_ref, live_ref, rows_ref, accept_ref):
    row_count = excess_ref.shape[0]
    seq_count, span = accept_ref.shape
    position = lax.broadcasted_iota(jnp.int32, (1, 128), 1) % span
    live = position < live_ref[...]
    excess_mass = jnp.sum(mass_ref[...], axis=0)
    scale = jnp.where(live, vocab_total / (excess_mass + 1e-06), 0.0)
    row = lax.broadcasted_iota(jnp.int32, (row_count, 128), 0)
    lane = lax.broadcasted_iota(jnp.int32, (row_count, 128), 1)
    column = jnp.sum(jnp.where(row == lane, scale, 0.0), axis=1, keepdims=True)
    rows_ref[...] = excess_ref[...] * column
    steps = jnp.where(live, jnp.minimum(ratio_ref[...], 0.0), 0.0)
    row = lax.broadcasted_iota(jnp.int32, (seq_count, 128), 0)
    lane = lax.broadcasted_iota(jnp.int32, (seq_count, 128), 1)
    total = jnp.zeros((seq_count, 1), f32)
    for k in range(span):
        at = lane == row * span + k
        total = total + jnp.sum(jnp.where(at, steps, 0.0), axis=1, keepdims=True)
        alive = jnp.sum(jnp.where(at & live, 1.0, 0.0), axis=1, keepdims=True)
        accept_ref[:, k : k + 1] = jnp.where(alive > 0.0, total, 0.0)


def finish(excess, mass, log_ratio, live_rows, vocab_total, seq_count, span):
    return pl.pallas_call(
        functools.partial(finish_kernel, float(vocab_total)),
        out_shape=(
            jax.ShapeDtypeStruct(excess.shape, f32),
            jax.ShapeDtypeStruct((seq_count, span), f32),
        ),
        compiler_params=pltpu.CompilerParams(vmem_limit_bytes=4 << 20),
        name="finish",
    )(excess, mass, log_ratio, live_rows)


def per_device(partials, residual, norm_gain, head_weight, draft_logits, draft_tokens, live_drafts):
    dps = lax.axis_size("dp")
    sections = lax.axis_size("section")
    cores = lax.axis_size("core")
    owners = lax.axis_size(tensor_axes)
    chips = owners // cores
    tensor_at = lax.axis_index(tensor_axes)
    core_at = lax.axis_index("core")
    rows, width = residual.shape
    feature_count = width * sections
    own_rows = rows // owners
    depth, vocab_slice = head_weight.shape
    seq_count, draft_span = draft_tokens.shape
    row_count = seq_count * draft_span

    draft_block = draft_logits[0, 0, 0]
    source_rows, draft_width = draft_block.shape
    group_size = draft_width // vocab_slice
    member = tensor_at % group_size

    def draft_piece(block, flip):
        return lax.dynamic_slice_in_dim(block, (member ^ flip) * vocab_slice, vocab_slice, 1)

    terms = partials[0]
    half = rows // cores
    kept = lax.dynamic_slice_in_dim(terms, core_at * half, half, 0)
    given = lax.dynamic_slice_in_dim(terms, (1 - core_at) * half, half, 0)
    beside = draft_piece(draft_block, 1)
    beside = jnp.pad(beside, ((0, 8 - source_rows), (0, width - vocab_slice)))
    got = lax.ppermute(
        jnp.concatenate([given, beside]), "core", [(i, cores - 1 - i) for i in range(cores)]
    )
    own_at = (core_at * chips + lax.axis_index("zy")) * own_rows
    own_residual = lax.dynamic_slice_in_dim(residual, own_at, own_rows, 0)
    lanes = width // 8
    own_residual = own_residual.reshape(own_rows, 8, lanes).astype(f32)
    gain = norm_gain.reshape(8, lanes).astype(f32)
    got, kept, own_residual, gain, draft_block, head_weight = lax.optimization_barrier(
        (got, kept, own_residual, gain, draft_block, head_weight)
    )
    arrived = [draft_piece(draft_block, 0), got[half : half + source_rows, :vocab_slice]]
    got = got[:half]
    pair = (kept.astype(f32) + got.astype(f32)).astype(f16)
    pair_sums = exchange(pair.reshape(chips, own_rows, 8, lanes), "zy")
    for flip in range(2, group_size):
        arrived.append(
            lax.ppermute(
                draft_piece(draft_block, flip), tensor_axes, [(i, i ^ flip) for i in range(owners)]
            )
        )
    arrived = jnp.stack(arrived)
    pair_sums, weight_top = lax.optimization_barrier((pair_sums, head_weight[: depth // 2]))
    layer_total = jnp.sum(pair_sums.astype(f32), axis=0)

    hidden = lax.reduce_precision(own_residual + layer_total, 8, 7)
    squares = lax.psum(jnp.sum(hidden * hidden, axis=(1, 2)), "section")
    factor = lax.rsqrt(squares / feature_count + norm_epsilon)
    normed_own = (hidden * factor[:, None, None] * gain[None]).astype(bf16)

    normed_own, arrived, draft_tokens, live_drafts, core_at, tensor_at, member = (
        lax.optimization_barrier(
            (normed_own, arrived, draft_tokens, live_drafts, core_at, tensor_at, member)
        )
    )

    by_block = jnp.transpose(normed_own.reshape(own_rows, dps, depth), (1, 0, 2))
    to_send = jnp.broadcast_to(by_block[:, None], (dps, chips, own_rows, depth))
    mine = exchange(to_send.reshape(dps * chips, own_rows, depth), ("dp", "zy"))
    mine = mine.reshape(dps, rows // cores, depth)
    mine, arrived, draft_tokens, live_drafts, core_at, tensor_at, member = (
        lax.optimization_barrier(
            (mine, arrived, draft_tokens, live_drafts, core_at, tensor_at, member)
        )
    )
    other = lax.ppermute(mine, "core", [(0, 1), (1, 0)])

    drafted = jnp.concatenate(
        [
            lax.dynamic_index_in_dim(arrived, member ^ source, 0, keepdims=False)
            for source in range(group_size)
        ]
    ).astype(f32)
    local_ids = draft_tokens.reshape(row_count) - tensor_at * vocab_slice
    live_rows = one_row(jnp.repeat(live_drafts, draft_span))

    def statistics(values):
        peak = jnp.max(values, axis=1)
        exps = jnp.exp(values - peak[:, None])
        chosen = lax.broadcasted_iota(jnp.int32, values.shape, 1) == local_ids[:, None]
        pick = jnp.sum(jnp.where(chosen, values, 0.0), axis=1)
        return exps, [peak, jnp.sum(exps, axis=1), pick]

    exp_draft, stats_draft = statistics(drafted)
    other, exp_draft, stats_draft, live_rows, local_ids = lax.optimization_barrier(
        (other, exp_draft, stats_draft, live_rows, local_ids)
    )

    normed = jnp.where(
        core_at == 0, jnp.stack([mine, other], axis=1), jnp.stack([other, mine], axis=1)
    ).reshape(dps * rows, depth)
    products = head_product(normed, weight_top, head_weight)
    products = products.astype(f16)

    by_dp = exchange(products, "dp").reshape(dps, rows, vocab_slice)

    by_dp = jnp.sum(by_dp.astype(f32), axis=0).astype(f16)
    gathered = exchange(by_dp, "section").reshape(sections, row_count, vocab_slice)
    logits = jnp.sum(gathered.astype(f32), axis=0)

    exp_target, stats_target = statistics(logits)
    stats = share(jnp.concatenate(stats_target + stats_draft))
    stats = stats[:, 0, : 6 * row_count].reshape(owners, 6, row_count)

    def combine(peaks, totals, picks, own_peak):
        peak = jnp.max(peaks, axis=0)
        total = jnp.sum(totals * jnp.exp(peaks - peak[None]), axis=0)
        return peak, total, jnp.sum(picks, axis=0), jnp.exp(own_peak - peak) / total

    peak_target, total_target, pick_target, scale_target = combine(
        stats[:, 0], stats[:, 1], stats[:, 2], stats_target[0]
    )
    peak_draft, total_draft, pick_draft, scale_draft = combine(
        stats[:, 3], stats[:, 4], stats[:, 5], stats_draft[0]
    )
    excess = jnp.maximum(
        exp_target * scale_target[:, None] - exp_draft * scale_draft[:, None], 0.0
    )
    log_ratio = (
        pick_target
        - peak_target
        - jnp.log(total_target)
        - (pick_draft - peak_draft - jnp.log(total_draft))
    )
    excess, log_ratio, live_rows = lax.optimization_barrier(
        (excess, one_row(log_ratio), live_rows)
    )
    mass = share(jnp.sum(excess, axis=1))
    return finish(
        excess, mass, log_ratio, live_rows, vocab_slice * owners, seq_count, draft_span
    )


def solution(mesh):
    sizes = mesh.shape
    split = Mesh(
        mesh.devices.reshape(sizes["dp"], sizes["tensor"] // 2, 2, sizes["section"]),
        ("dp",) + tensor_axes + ("section",),
    )
    return jax.shard_map(
        per_device,
        mesh=split,
        in_specs=(
            P(tensor_axes, "dp", "section"),
            P("dp", "section"),
            P("section"),
            P(("section", "dp"), tensor_axes),
            P("dp", "section", tensor_axes, None, None),
            P(("dp", "section"), None),
            P(("dp", "section")),
        ),
        out_specs=(P(("dp", "section"), tensor_axes), P(("dp", "section"), None)),
        check_vma=False,
    )
```

time: 139 us -> 129 us (0.928)
  blocking collectives: 33.7 us -> 88.8 us
  waiting for transfers between devices: 45.8 us -> 2.71 us
  starting transfers between devices: 42.3 us -> 23.9 us
  other arithmetic: 7.45 us -> 3.07 us
    all_to_all x1 -> x5, blocking collectives: 19 us -> 74.6 us  [exchange(): return lax.all_to_all(blocks, axis, split_axis=0, concat_axis=0, tiled=True)]
    all_to_all x5 -> x1, waiting for transfers between devices: 44.7 us -> 2.29 us  [exchange(): return lax.all_to_all(blocks, axis, split_axis=0, concat_axis=0, tiled=True)]
    all_to_all x5 -> x1, starting transfers between devices: 28.5 us -> 3.53 us  [exchange(): return lax.all_to_all(blocks, axis, split_axis=0, concat_axis=0, tiled=True)]
    ppermute x3, starting transfers between devices: 7.88 us -> 14.3 us  [the longest x1 8.79 us: per_device(): lax.ppermute(jnp.concatenate([given, beside]), 'core', [(i, cores - 1 - i...]
    another operation x2 -> x3, local copies, waits for them, and re-layouts: 2.27 us -> 0.12 us  [the longest x1 0.09 us: one_row(): return jnp.pad(values[None], ((0, 0), (0, 128 - values.shape[0])))]
    dynamic_slice x1 -> x2, local copies, waits for them, and re-layouts: 0.03 us -> 1.82 us  [the longest x1 1.06 us: per_device(): kept = lax.dynamic_slice_in_dim(terms, core_at * half, half, 0)]
    slice x0 -> x1, local copies, waits for them, and re-layouts: none -> 1.73 us  [per_device(): head_weight[:depth // 2]]
    pallas_call x1 -> x2, Pallas kernels: 1.84 us -> 2.8 us  [the longest x1 2.01 us: head_product(): pl.pallas_call(head_kernel, in_specs=[pl.BlockSpec(memory_space=pltpu.VME...]
  transfers between devices with their start and end apart: 9 -> 5, of which waited for: 6 -> 2; matrix products, arithmetic and copies ran while one was open for 2% -> 3% of each run, Pallas kernels for 0% -> 0%
where the time goes in v3:
time: 129 us; the launch traced here: 128 us
  blocking collectives  88.8 us (69%)
  starting transfers between devices  23.9 us (19%)
  local copies, waits for them, and re-layouts  5.89 us (5%)
  other arithmetic  3.07 us (2%)
  Pallas kernels  2.8 us (2%)
  waiting for transfers between devices  2.71 us (2%)
    all_to_all x5, blocking collectives, exchange(): return lax.all_to_all(blocks, axis, split_axis=0, concat_axis=0, tiled=True)  74.6 us
    psum x1, blocking collectives, per_device(): squares = lax.psum(jnp.sum(hidden * hidden, axis=(1, 2)), 'section')  14.2 us
    ppermute x1, starting transfers between devices, per_device(): lax.ppermute(jnp.concatenate([given, beside]), 'core', [(i, cores - 1 - i...  8.79 us
    ppermute x1, starting transfers between devices, per_device(): other = lax.ppermute(mine, 'core', [(0, 1), (1, 0)])  6.14 us
    ppermute x2, starting transfers between devices, per_device(): lax.ppermute(draft_piece(draft_block, flip), tensor_axes, [(i, i ^ flip)...  5.48 us
    all_to_all x1, starting transfers between devices, exchange(): return lax.all_to_all(blocks, axis, split_axis=0, concat_axis=0, tiled=True)  3.53 us
  transfers between devices with their start and end apart: 5, of which 2 were waited for; matrix products, arithmetic and copies ran while one was open for 3% of the time, Pallas kernels for 0%

profile of v3, /device:TPU:1, one launch (start us, length us, event | category | flops | bytes accessed | tf_op | source)
XLA Modules:
  0.0 128.3 jit_solution(14041127601773926572)
XLA Ops:
  0.7 0.8 dynamic-slice_bitcast_fusion.7
  1.4 1.1 dynamic-slice_bitcast_fusion
  2.5 8.8 %collective-permute-start = (bf16[40,4096]{1,0:T(8,128)(2,1)S(1)}, bf16[40,4096]{1,0:T(8,128)(2,1)S(1)}, u32[]{:S(2)}, u32[]{:S(2)}) collective-permute-start(bf16[40,4096]{1,0:T(8,128)(2,1)S(1)} %fusion.1), channel_id=1, source_target_pairs={{0,4},{4,0},{1,5},{5,1},{2,6},{6,2},{3,7},{7,3},{8,12},{12,8},{9,1... | collective-permute-start | bytes 983048 | tf_op jit(solution)/shard_map/ppermute | solution.py:133
  11.3 0.7 reshape.131
  12.1 0.9 dynamic-slice_convert_fusion
  13.1 0.8 copy.19
  13.9 3.5 %all-to-all-start = ((f16[16,2,8,512]{3,2,1,0:T(8,128)(2,1)}), f16[16,2,8,512]{3,2,1,0:T(8,128)(2,1)S(1)}, u32[]{:S(2)}, u32[]{:S(2)}) async-start(f16[16,2,8,512]{3,2,1,0:T(8,128)(2,1)} %bitcast.33), calls=%async_computation | async-start | bytes 524288 | tf_op jit(solution)/shard_map/all_to_all | solution.py:18
  17.4 3.6 %collective-permute-start.2 = (bf16[4,2048]{1,0:T(4,128)(2,1)S(1)}, bf16[4,2048]{1,0:T(4,128)(2,1)S(1)}, u32[]{:S(2)}, u32[]{:S(2)}) collective-permute-start(bf16[4,2048]{1,0:T(4,128)(2,1)S(1)} %get-tuple-element.84), channel_id=1, source_target_pairs={{0,12},{4,8},{8,4},{12,0},{16,28},{20,24},{24,20},{28,16},{32,44},... | collective-permute-start | bytes 49160 | tf_op jit(solution)/shard_map/ppermute | solution.py:150
  21.0 1.9 %collective-permute-start.1 = (bf16[4,2048]{1,0:T(4,128)(2,1)S(1)}, bf16[4,2048]{1,0:T(4,128)(2,1)S(1)}, u32[]{:S(2)}, u32[]{:S(2)}) collective-permute-start(bf16[4,2048]{1,0:T(4,128)(2,1)S(1)} %get-tuple-element.85), channel_id=1, source_target_pairs={{0,8},{4,12},{8,0},{12,4},{16,24},{20,28},{24,16},{28,20},{32,40},... | collective-permute-start | bytes 49160 | tf_op jit(solution)/shard_map/ppermute | solution.py:150
  22.9 1.7 %slice.31.top_ref = bf16[512,2048]{1,0:T(8,128)(2,1)S(1)} slice(bf16[1024,2048]{1,0:T(8,128)(2,1)} %w_hbm), slice={[0:512], [0:2048]} | slice | bytes 4194304 | tf_op jit(solution)/shard_map/slice | solution.py:155
  24.7 2.3 %all-to-all-done = f16[16,2,8,512]{3,2,1,0:T(8,128)(2,1)S(1)} async-done(((f16[16,2,8,512]{3,2,1,0:T(8,128)(2,1)}), f16[16,2,8,512]{3,2,1,0:T(8,128)(2,1)S(1)}, u32[]{:S(2)}, u32[]{:S(2)}) %all-to-all-start) | async-done | bytes 262176 | tf_op jit(solution)/shard_map/all_to_all | solution.py:18
  27.0 0.1 multiply_reduce_fusion
  27.2 14.2 %psum.7 = f32[2]{0:T(128)S(1)} all-reduce(f32[2]{0:T(128)S(1)} %multiply_reduce_fusion), channel_id=1, replica_groups=mesh['dp'=4,'zy'=16,'core'=2,'section'=4] {'section'}, use_global_device_ids=true, to_apply=%region_2.3 | all-reduce | flops 2 | bytes 16 | tf_op jit(solution)/shard_map/psum | solution.py:159
  41.6 0.1 broadcast_in_dim.21
  41.7 20.1 %all_to_all.35 = bf16[64,2,1024]{2,1,0:T(2,128)(2,1)S(1)} all-to-all(bf16[64,2,1024]{2,1,0:T(2,128)(2,1)S(1)} %bitcast.73), channel_id=1, replica_groups=mesh['dp'=4,'zy'=16,'core'=2,'section'=4] {'dp','zy'}, dimensions={0} | all-to-all | bytes 524288 | tf_op jit(solution)/shard_map/all_to_all | solution.py:18
  62.0 6.1 %collective-permute-start.3 = (bf16[4,32,1024]{2,1,0:T(8,128)(2,1)S(1)}, bf16[4,32,1024]{2,1,0:T(8,128)(2,1)S(1)}, u32[]{:S(2)}, u32[]{:S(2)}) collective-permute-start(bf16[4,32,1024]{2,1,0:T(8,128)(2,1)S(1)} %reshape.129), channel_id=1, source_target_pairs={{0,4},{4,0},{1,5},{5,1},{2,6},{6,2},{3,7},{7,3},{8,12},{12,8},{9,1... | collective-permute-start | bytes 786440 | tf_op jit(solution)/shard_map/ppermute | solution.py:178
  68.2 0.2 fusion.12
  68.6 0.2 fusion.3
  68.8 0.4 collective-permute-done.3
  69.3 2.0 %head_product.1 = f32[256,2048]{1,0:T(8,128)S(1)} custom-call(bf16[256,1024]{1,0:T(8,128)(2,1)S(1)} %bitcast.69, bf16[512,2048]{1,0:T(8,128)(2,1)S(1)} %slice.31.top_ref, bf16[1024,2048]{1,0:T(8,128)(2,1)} %w_hbm), custom_call_target="tpu_custom_call" | custom-call | tf_op jit(solution)/shard_map/head_product/pallas_call | solution.py:55
  71.3 0.1 convert_element_type.63
  71.5 17.3 %all_to_all.36 = f16[4,64,2048]{2,1,0:T(8,128)(2,1)S(1)} all-to-all(f16[4,64,2048]{2,1,0:T(8,128)(2,1)S(1)} %bitcast.70), channel_id=1, replica_groups=mesh['dp'=4,'zy'=16,'core'=2,'section'=4] {'dp'}, dimensions={0} | all-to-all | bytes 2097152 | tf_op jit(solution)/shard_map/all_to_all | solution.py:18
  88.7 0.2 convert_reduce_fusion
  89.0 11.3 %all_to_all.37 = f16[4,16,2048]{2,1,0:T(8,128)(2,1)S(1)} all-to-all(f16[4,16,2048]{2,1,0:T(8,128)(2,1)S(1)} %bitcast.72), channel_id=1, replica_groups=mesh['dp'=4,'zy'=16,'core'=2,'section'=4] {'section'}, dimensions={0} | all-to-all | bytes 524288 | tf_op jit(solution)/shard_map/all_to_all | solution.py:18
  100.3 0.1 reduce_max.43
  100.5 0.2 select_reduce_fusion
  100.8 14.6 %all_to_all.38 = f32[32,1,128]{2,1,0:T(1,128)S(1)} all-to-all(f32[32,1,128]{2,1,0:T(1,128)S(1)} %broadcast_in_dim.26), channel_id=1, replica_groups=mesh['dp'=4,'zy'=16,'core'=2,'section'=4] {'zy','core'}, dimensions={0} | all-to-all | bytes 32768 | tf_op jit(solution)/shard_map/all_to_all | solution.py:18
  115.5 0.1 slice_reduce_fusion.1
  115.6 0.2 fusion.8
  116.0 0.1 reduce_sum.129
  116.1 11.4 %all_to_all.39.mass_ref = f32[32,1,128]{2,1,0:T(1,128)S(1)} all-to-all(f32[32,1,128]{2,1,0:T(1,128)S(1)} %broadcast_in_dim.55), channel_id=1, replica_groups=mesh['dp'=4,'zy'=16,'core'=2,'section'=4] {'zy','core'}, dimensions={0} | all-to-all | bytes 32768 | tf_op jit(solution)/shard_map/all_to_all | solution.py:18
  127.5 0.8 finish.1
  (40 shorter events, 1.2 us)
Async XLA Ops:
  0.6 16.8 %copy-start = (bf16[1,1,1,4,8192]{4,3,2,1,0:T(4,128)(2,1)S(1)}, bf16[1,1,1,4,8192]{4,3,2,1,0:T(4,128)(2,1)}, u32[]{:S(2)}) copy-start(bf16[1,1,1,4,8192]{4,3,2,1,0:T(4,128)(2,1)} %param.11) | copy-start | bytes 196612
  2.5 10.4 %collective-permute-start = (bf16[40,4096]{1,0:T(8,128)(2,1)S(1)}, bf16[40,4096]{1,0:T(8,128)(2,1)S(1)}, u32[]{:S(2)}, u32[]{:S(2)}) collective-permute-start(bf16[40,4096]{1,0:T(8,128)(2,1)S(1)} %fusion.1), channel_id=1, source_target_pairs={{0,4},{4,0},{1,5},{5,1},{2,6},{6,2},{3,7},{7,3},{8,12},{12,8},{9,1... | collective-permute-start | bytes 983048 | tf_op jit(solution)/shard_map/ppermute | solution.py:133
  13.9 13.1 %all-to-all-start = ((f16[16,2,8,512]{3,2,1,0:T(8,128)(2,1)}), f16[16,2,8,512]{3,2,1,0:T(8,128)(2,1)S(1)}, u32[]{:S(2)}, u32[]{:S(2)}) async-start(f16[16,2,8,512]{3,2,1,0:T(8,128)(2,1)} %bitcast.33), calls=%async_computation | async-start | bytes 524288 | tf_op jit(solution)/shard_map/all_to_all | solution.py:18
  17.4 9.7 %collective-permute-start.2 = (bf16[4,2048]{1,0:T(4,128)(2,1)S(1)}, bf16[4,2048]{1,0:T(4,128)(2,1)S(1)}, u32[]{:S(2)}, u32[]{:S(2)}) collective-permute-start(bf16[4,2048]{1,0:T(4,128)(2,1)S(1)} %get-tuple-element.84), channel_id=1, source_target_pairs={{0,12},{4,8},{8,4},{12,0},{16,28},{20,24},{24,20},{28,16},{32,44},... | collective-permute-start | bytes 49160 | tf_op jit(solution)/shard_map/ppermute | solution.py:150
  21.0 6.1 %collective-permute-start.1 = (bf16[4,2048]{1,0:T(4,128)(2,1)S(1)}, bf16[4,2048]{1,0:T(4,128)(2,1)S(1)}, u32[]{:S(2)}, u32[]{:S(2)}) collective-permute-start(bf16[4,2048]{1,0:T(4,128)(2,1)S(1)} %get-tuple-element.85), channel_id=1, source_target_pairs={{0,8},{4,12},{8,0},{12,4},{16,24},{20,28},{24,16},{28,20},{32,40},... | collective-permute-start | bytes 49160 | tf_op jit(solution)/shard_map/ppermute | solution.py:150
  24.7 43.5 %copy-start.1 = (s32[4,4]{1,0:T(4,128)S(1)}, s32[4,4]{1,0:T(4,128)}, u32[]{:S(2)}) copy-start(s32[4,4]{1,0:T(4,128)} %param.12) | copy-start | bytes 196
  24.7 43.8 %copy-start.2 = (s32[4]{0:T(128)S(1)}, s32[4]{0:T(128)}, u32[]{:S(2)}) copy-start(s32[4]{0:T(128)} %param.13) | copy-start | bytes 52
  62.0 7.3 %collective-permute-start.3 = (bf16[4,32,1024]{2,1,0:T(8,128)(2,1)S(1)}, bf16[4,32,1024]{2,1,0:T(8,128)(2,1)S(1)}, u32[]{:S(2)}, u32[]{:S(2)}) collective-permute-start(bf16[4,32,1024]{2,1,0:T(8,128)(2,1)S(1)} %reshape.129), channel_id=1, source_target_pairs={{0,4},{4,0},{1,5},{5,1},{2,6},{6,2},{3,7},{7,3},{8,12},{12,8},{9,1... | collective-permute-start | bytes 786440 | tf_op jit(solution)/shard_map/ppermute | solution.py:178

commit v4 on v3

--- a/solution.py
+++ b/solution.py
@@ -11,6 +11,9 @@
 f32 = jnp.float32
 bf16 = jnp.bfloat16
 f16 = jnp.float16
+pair_scale = 8192.0
+block_scale = 32.0
+dp_scale = 16.0
 tensor_axes = ("zy", "core")
 
 
@@ -143,7 +146,7 @@
     )
     arrived = [draft_piece(draft_block, 0), got[half : half + source_rows, :vocab_slice]]
     got = got[:half]
-    pair = (kept.astype(f32) + got.astype(f32)).astype(f16)
+    pair = ((kept.astype(f32) + got.astype(f32)) * pair_scale).astype(f16)
     pair_sums = exchange(pair.reshape(chips, own_rows, 8, lanes), "zy")
     for flip in range(2, group_size):
         arrived.append(
@@ -153,7 +156,7 @@
         )
     arrived = jnp.stack(arrived)
     pair_sums, weight_top = lax.optimization_barrier((pair_sums, head_weight[: depth // 2]))
-    layer_total = jnp.sum(pair_sums.astype(f32), axis=0)
+    layer_total = jnp.sum(pair_sums.astype(f32), axis=0) * (1.0 / pair_scale)
 
     hidden = lax.reduce_precision(own_residual + layer_total, 8, 7)
     squares = lax.psum(jnp.sum(hidden * hidden, axis=(1, 2)), "section")
@@ -202,13 +205,13 @@
         core_at == 0, jnp.stack([mine, other], axis=1), jnp.stack([other, mine], axis=1)
     ).reshape(dps * rows, depth)
     products = head_product(normed, weight_top, head_weight)
-    products = products.astype(f16)
+    products = (products * block_scale).astype(f16)
 
     by_dp = exchange(products, "dp").reshape(dps, rows, vocab_slice)
 
-    by_dp = jnp.sum(by_dp.astype(f32), axis=0).astype(f16)
+    by_dp = (jnp.sum(by_dp.astype(f32), axis=0) * (dp_scale / block_scale)).astype(f16)
     gathered = exchange(by_dp, "section").reshape(sections, row_count, vocab_slice)
-    logits = jnp.sum(gathered.astype(f32), axis=0)
+    logits = jnp.sum(gathered.astype(f32), axis=0) * (1.0 / dp_scale)
 
     exp_target, stats_target = statistics(logits)
     stats = share(jnp.concatenate(stats_target + stats_draft))

time: 129 us -> 129 us (level)
  no operation moved by 1% of the time
where the time goes in v4:
time: 129 us; the launch traced here: 128 us
  blocking collectives  88.8 us (69%)
  starting transfers between devices  23.9 us (19%)
  local copies, waits for them, and re-layouts  5.89 us (5%)
  other arithmetic  3.16 us (2%)
  Pallas kernels  2.8 us (2%)
  waiting for transfers between devices  2.71 us (2%)
    all_to_all x5, blocking collectives, exchange(): return lax.all_to_all(blocks, axis, split_axis=0, concat_axis=0, tiled=True)  74.6 us
    psum x1, blocking collectives, per_device(): squares = lax.psum(jnp.sum(hidden * hidden, axis=(1, 2)), 'section')  14.2 us
    ppermute x1, starting transfers between devices, per_device(): lax.ppermute(jnp.concatenate([given, beside]), 'core', [(i, cores - 1 - i...  8.79 us
    ppermute x1, starting transfers between devices, per_device(): other = lax.ppermute(mine, 'core', [(0, 1), (1, 0)])  6.14 us
    ppermute x2, starting transfers between devices, per_device(): lax.ppermute(draft_piece(draft_block, flip), tensor_axes, [(i, i ^ flip)...  5.48 us
    all_to_all x1, starting transfers between devices, exchange(): return lax.all_to_all(blocks, axis, split_axis=0, concat_axis=0, tiled=True)  3.53 us
  transfers between devices with their start and end apart: 5, of which 2 were waited for; matrix products, arithmetic and copies ran while one was open for 3% of the time, Pallas kernels for 0%

profile of v4, /device:TPU:1, one launch (start us, length us, event | category | flops | bytes accessed | tf_op | source)
XLA Modules:
  0.0 128.3 jit_solution(14582823348468085527)
XLA Ops:
  0.7 0.8 dynamic-slice_bitcast_fusion.7
  1.4 1.1 dynamic-slice_bitcast_fusion
  2.5 8.8 %collective-permute-start = (bf16[40,4096]{1,0:T(8,128)(2,1)S(1)}, bf16[40,4096]{1,0:T(8,128)(2,1)S(1)}, u32[]{:S(2)}, u32[]{:S(2)}) collective-permute-start(bf16[40,4096]{1,0:T(8,128)(2,1)S(1)} %fusion.1), channel_id=1, source_target_pairs={{0,4},{4,0},{1,5},{5,1},{2,6},{6,2},{3,7},{7,3},{8,12},{12,8},{9,1... | collective-permute-start | bytes 983048 | tf_op jit(solution)/shard_map/ppermute | solution.py:136
  11.3 0.7 reshape.133
  12.1 0.9 dynamic-slice_convert_fusion
  13.1 0.8 copy.19
  13.9 3.5 %all-to-all-start = ((f16[16,2,8,512]{3,2,1,0:T(8,128)(2,1)}), f16[16,2,8,512]{3,2,1,0:T(8,128)(2,1)S(1)}, u32[]{:S(2)}, u32[]{:S(2)}) async-start(f16[16,2,8,512]{3,2,1,0:T(8,128)(2,1)} %bitcast.33), calls=%async_computation | async-start | bytes 524288 | tf_op jit(solution)/shard_map/all_to_all | solution.py:21
  17.5 3.6 %collective-permute-start.2 = (bf16[4,2048]{1,0:T(4,128)(2,1)S(1)}, bf16[4,2048]{1,0:T(4,128)(2,1)S(1)}, u32[]{:S(2)}, u32[]{:S(2)}) collective-permute-start(bf16[4,2048]{1,0:T(4,128)(2,1)S(1)} %get-tuple-element.84), channel_id=1, source_target_pairs={{0,12},{4,8},{8,4},{12,0},{16,28},{20,24},{24,20},{28,16},{32,44},... | collective-permute-start | bytes 49160 | tf_op jit(solution)/shard_map/ppermute | solution.py:153
  21.0 1.9 %collective-permute-start.1 = (bf16[4,2048]{1,0:T(4,128)(2,1)S(1)}, bf16[4,2048]{1,0:T(4,128)(2,1)S(1)}, u32[]{:S(2)}, u32[]{:S(2)}) collective-permute-start(bf16[4,2048]{1,0:T(4,128)(2,1)S(1)} %get-tuple-element.85), channel_id=1, source_target_pairs={{0,8},{4,12},{8,0},{12,4},{16,24},{20,28},{24,16},{28,20},{32,40},... | collective-permute-start | bytes 49160 | tf_op jit(solution)/shard_map/ppermute | solution.py:153
  23.0 1.7 %slice.31.top_ref = bf16[512,2048]{1,0:T(8,128)(2,1)S(1)} slice(bf16[1024,2048]{1,0:T(8,128)(2,1)} %w_hbm), slice={[0:512], [0:2048]} | slice | bytes 4194304 | tf_op jit(solution)/shard_map/slice | solution.py:158
  24.7 2.3 %all-to-all-done = f16[16,2,8,512]{3,2,1,0:T(8,128)(2,1)S(1)} async-done(((f16[16,2,8,512]{3,2,1,0:T(8,128)(2,1)}), f16[16,2,8,512]{3,2,1,0:T(8,128)(2,1)S(1)}, u32[]{:S(2)}, u32[]{:S(2)}) %all-to-all-start) | async-done | bytes 262176 | tf_op jit(solution)/shard_map/all_to_all | solution.py:21
  27.1 0.1 multiply_reduce_fusion.1
  27.2 14.2 %psum.7 = f32[2]{0:T(128)S(1)} all-reduce(f32[2]{0:T(128)S(1)} %multiply_reduce_fusion.1), channel_id=1, replica_groups=mesh['dp'=4,'zy'=16,'core'=2,'section'=4] {'section'}, use_global_device_ids=true, to_apply=%region_2.3 | all-reduce | flops 2 | bytes 16 | tf_op jit(solution)/shard_map/psum | solution.py:162
  41.6 0.1 broadcast_in_dim.21
  41.7 20.1 %all_to_all.35 = bf16[64,2,1024]{2,1,0:T(2,128)(2,1)S(1)} all-to-all(bf16[64,2,1024]{2,1,0:T(2,128)(2,1)S(1)} %bitcast.73), channel_id=1, replica_groups=mesh['dp'=4,'zy'=16,'core'=2,'section'=4] {'dp','zy'}, dimensions={0} | all-to-all | bytes 524288 | tf_op jit(solution)/shard_map/all_to_all | solution.py:21
  62.0 6.1 %collective-permute-start.3 = (bf16[4,32,1024]{2,1,0:T(8,128)(2,1)S(1)}, bf16[4,32,1024]{2,1,0:T(8,128)(2,1)S(1)}, u32[]{:S(2)}, u32[]{:S(2)}) collective-permute-start(bf16[4,32,1024]{2,1,0:T(8,128)(2,1)S(1)} %reshape.131), channel_id=1, source_target_pairs={{0,4},{4,0},{1,5},{5,1},{2,6},{6,2},{3,7},{7,3},{8,12},{12,8},{9,1... | collective-permute-start | bytes 786440 | tf_op jit(solution)/shard_map/ppermute | solution.py:181
  68.2 0.2 fusion.12
  68.6 0.2 fusion.3
  68.9 0.4 collective-permute-done.3
  69.3 2.0 %head_product.1 = f32[256,2048]{1,0:T(8,128)S(1)} custom-call(bf16[256,1024]{1,0:T(8,128)(2,1)S(1)} %bitcast.69, bf16[512,2048]{1,0:T(8,128)(2,1)S(1)} %slice.31.top_ref, bf16[1024,2048]{1,0:T(8,128)(2,1)} %w_hbm), custom_call_target="tpu_custom_call" | custom-call | tf_op jit(solution)/shard_map/head_product/pallas_call | solution.py:58
  71.3 0.2 multiply_convert_fusion
  71.5 17.3 %all_to_all.36 = f16[4,64,2048]{2,1,0:T(8,128)(2,1)S(1)} all-to-all(f16[4,64,2048]{2,1,0:T(8,128)(2,1)S(1)} %bitcast.70), channel_id=1, replica_groups=mesh['dp'=4,'zy'=16,'core'=2,'section'=4] {'dp'}, dimensions={0} | all-to-all | bytes 2097152 | tf_op jit(solution)/shard_map/all_to_all | solution.py:21
  88.8 0.2 convert_reduce_fusion
  89.1 11.3 %all_to_all.37 = f16[4,16,2048]{2,1,0:T(8,128)(2,1)S(1)} all-to-all(f16[4,16,2048]{2,1,0:T(8,128)(2,1)S(1)} %bitcast.72), channel_id=1, replica_groups=mesh['dp'=4,'zy'=16,'core'=2,'section'=4] {'section'}, dimensions={0} | all-to-all | bytes 524288 | tf_op jit(solution)/shard_map/all_to_all | solution.py:21
  100.4 0.1 multiply_reduce_fusion
  100.5 0.2 select_reduce_fusion
  100.9 14.6 %all_to_all.38 = f32[32,1,128]{2,1,0:T(1,128)S(1)} all-to-all(f32[32,1,128]{2,1,0:T(1,128)S(1)} %broadcast_in_dim.26), channel_id=1, replica_groups=mesh['dp'=4,'zy'=16,'core'=2,'section'=4] {'zy','core'}, dimensions={0} | all-to-all | bytes 32768 | tf_op jit(solution)/shard_map/all_to_all | solution.py:21
  115.5 0.1 slice_reduce_fusion.1
  115.7 0.2 fusion.8
  116.0 0.1 reduce_sum.129
  116.2 11.4 %all_to_all.39.mass_ref = f32[32,1,128]{2,1,0:T(1,128)S(1)} all-to-all(f32[32,1,128]{2,1,0:T(1,128)S(1)} %broadcast_in_dim.55), channel_id=1, replica_groups=mesh['dp'=4,'zy'=16,'core'=2,'section'=4] {'zy','core'}, dimensions={0} | all-to-all | bytes 32768 | tf_op jit(solution)/shard_map/all_to_all | solution.py:21
  127.6 0.8 finish.1
  (40 shorter events, 1.3 us)
Async XLA Ops:
  0.6 16.8 %copy-start = (bf16[1,1,1,4,8192]{4,3,2,1,0:T(4,128)(2,1)S(1)}, bf16[1,1,1,4,8192]{4,3,2,1,0:T(4,128)(2,1)}, u32[]{:S(2)}) copy-start(bf16[1,1,1,4,8192]{4,3,2,1,0:T(4,128)(2,1)} %param.11) | copy-start | bytes 196612
  2.5 10.4 %collective-permute-start = (bf16[40,4096]{1,0:T(8,128)(2,1)S(1)}, bf16[40,4096]{1,0:T(8,128)(2,1)S(1)}, u32[]{:S(2)}, u32[]{:S(2)}) collective-permute-start(bf16[40,4096]{1,0:T(8,128)(2,1)S(1)} %fusion.1), channel_id=1, source_target_pairs={{0,4},{4,0},{1,5},{5,1},{2,6},{6,2},{3,7},{7,3},{8,12},{12,8},{9,1... | collective-permute-start | bytes 983048 | tf_op jit(solution)/shard_map/ppermute | solution.py:136
  13.9 13.1 %all-to-all-start = ((f16[16,2,8,512]{3,2,1,0:T(8,128)(2,1)}), f16[16,2,8,512]{3,2,1,0:T(8,128)(2,1)S(1)}, u32[]{:S(2)}, u32[]{:S(2)}) async-start(f16[16,2,8,512]{3,2,1,0:T(8,128)(2,1)} %bitcast.33), calls=%async_computation | async-start | bytes 524288 | tf_op jit(solution)/shard_map/all_to_all | solution.py:21
  17.5 9.7 %collective-permute-start.2 = (bf16[4,2048]{1,0:T(4,128)(2,1)S(1)}, bf16[4,2048]{1,0:T(4,128)(2,1)S(1)}, u32[]{:S(2)}, u32[]{:S(2)}) collective-permute-start(bf16[4,2048]{1,0:T(4,128)(2,1)S(1)} %get-tuple-element.84), channel_id=1, source_target_pairs={{0,12},{4,8},{8,4},{12,0},{16,28},{20,24},{24,20},{28,16},{32,44},... | collective-permute-start | bytes 49160 | tf_op jit(solution)/shard_map/ppermute | solution.py:153
  21.0 6.2 %collective-permute-start.1 = (bf16[4,2048]{1,0:T(4,128)(2,1)S(1)}, bf16[4,2048]{1,0:T(4,128)(2,1)S(1)}, u32[]{:S(2)}, u32[]{:S(2)}) collective-permute-start(bf16[4,2048]{1,0:T(4,128)(2,1)S(1)} %get-tuple-element.85), channel_id=1, source_target_pairs={{0,8},{4,12},{8,0},{12,4},{16,24},{20,28},{24,16},{28,20},{32,40},... | collective-permute-start | bytes 49160 | tf_op jit(solution)/shard_map/ppermute | solution.py:153
  24.7 43.5 %copy-start.1 = (s32[4,4]{1,0:T(4,128)S(1)}, s32[4,4]{1,0:T(4,128)}, u32[]{:S(2)}) copy-start(s32[4,4]{1,0:T(4,128)} %param.12) | copy-start | bytes 196
  24.7 43.8 %copy-start.2 = (s32[4]{0:T(128)S(1)}, s32[4]{0:T(128)}, u32[]{:S(2)}) copy-start(s32[4]{0:T(128)} %param.13) | copy-start | bytes 52
  62.0 7.3 %collective-permute-start.3 = (bf16[4,32,1024]{2,1,0:T(8,128)(2,1)S(1)}, bf16[4,32,1024]{2,1,0:T(8,128)(2,1)S(1)}, u32[]{:S(2)}, u32[]{:S(2)}) collective-permute-start(bf16[4,32,1024]{2,1,0:T(8,128)(2,1)S(1)} %reshape.131), channel_id=1, source_target_pairs={{0,4},{4,0},{1,5},{5,1},{2,6},{6,2},{3,7},{7,3},{8,12},{12,8},{9,1... | collective-permute-start | bytes 786440 | tf_op jit(solution)/shard_map/ppermute | solution.py:181

commit v5 on v4

--- a/solution.py
+++ b/solution.py
@@ -21,13 +21,11 @@
     return lax.all_to_all(blocks, axis, split_axis=0, concat_axis=0, tiled=True)
 
 
+share_axes = tensor_axes[::-1]
+
+
 def one_row(values):
     return jnp.pad(values[None], ((0, 0), (0, 128 - values.shape[0])))
-
-
-def share(values):
-    copies = lax.axis_size(tensor_axes)
-    return exchange(jnp.broadcast_to(one_row(values)[None], (copies, 1, 128)), tensor_axes)
 
 
 def head_kernel(x_ref, top_ref, w_hbm, o_ref, bottom, arrived):
@@ -68,6 +66,48 @@
         compiler_params=pltpu.CompilerParams(vmem_limit_bytes=48 << 20),
         name="head_product",
     )(x, top, w)
+
+
+def excess_kernel(stats_ref, own_ref, target_ref, draft_ref, excess_ref, mass_ref, ratio_ref):
+    rows = target_ref.shape[0]
+    stats = stats_ref[:, 0, :]
+
+    def turn(values, lanes):
+        return pltpu.roll(jnp.broadcast_to(values, (8, 128)), lanes % 128, 1)[:1]
+
+    peak = jnp.max(stats, axis=0, keepdims=True)
+    weights = pltpu.roll(jnp.exp(stats - peak), rows, 1)
+    total = jnp.sum(stats * weights, axis=0, keepdims=True)
+    pick = jnp.sum(stats, axis=0, keepdims=True)
+    scale = turn(jnp.exp(own_ref[...] - peak), rows) / total
+    log_prob = turn(pick, -2 * rows) - peak - jnp.log(turn(total, -rows))
+    ratio_ref[...] = log_prob - turn(log_prob, -3 * rows)
+    row = lax.broadcasted_iota(jnp.int32, (rows, 128), 0)
+    lane = lax.broadcasted_iota(jnp.int32, (rows, 128), 1)
+
+    def column(first):
+        return jnp.sum(jnp.where(lane == row + first, scale, 0.0), axis=1, keepdims=True)
+
+    excess = jnp.maximum(
+        target_ref[...] * column(rows) - draft_ref[...] * column(4 * rows), 0.0
+    )
+    excess_ref[...] = excess
+    mass = jnp.sum(excess, axis=1, keepdims=True)
+    mass = jnp.sum(jnp.where(lane == row, mass, 0.0), axis=0, keepdims=True)
+    mass_ref[...] = jnp.broadcast_to(mass[None], mass_ref.shape)
+
+
+def excess_of(stats, own, exp_target, exp_draft):
+    return pl.pallas_call(
+        excess_kernel,
+        out_shape=(
+            jax.ShapeDtypeStruct(exp_target.shape, f32),
+            jax.ShapeDtypeStruct(stats.shape, f32),
+            jax.ShapeDtypeStruct(own.shape, f32),
+        ),
+        compiler_params=pltpu.CompilerParams(vmem_limit_bytes=4 << 20),
+        name="excess",
+    )(stats, own, exp_target, exp_draft)
 
 
 def finish_kernel(vocab_total, excess_ref, mass_ref, ratio_ref, live_ref, rows_ref, accept_ref):
@@ -214,33 +254,10 @@
     logits = jnp.sum(gathered.astype(f32), axis=0) * (1.0 / dp_scale)
 
     exp_target, stats_target = statistics(logits)
-    stats = share(jnp.concatenate(stats_target + stats_draft))
-    stats = stats[:, 0, : 6 * row_count].reshape(owners, 6, row_count)
-
-    def combine(peaks, totals, picks, own_peak):
-        peak = jnp.max(peaks, axis=0)
-        total = jnp.sum(totals * jnp.exp(peaks - peak[None]), axis=0)
-        return peak, total, jnp.sum(picks, axis=0), jnp.exp(own_peak - peak) / total
-
-    peak_target, total_target, pick_target, scale_target = combine(
-        stats[:, 0], stats[:, 1], stats[:, 2], stats_target[0]
-    )
-    peak_draft, total_draft, pick_draft, scale_draft = combine(
-        stats[:, 3], stats[:, 4], stats[:, 5], stats_draft[0]
-    )
-    excess = jnp.maximum(
-        exp_target * scale_target[:, None] - exp_draft * scale_draft[:, None], 0.0
-    )
-    log_ratio = (
-        pick_target
-        - peak_target
-        - jnp.log(total_target)
-        - (pick_draft - peak_draft - jnp.log(total_draft))
-    )
-    excess, log_ratio, live_rows = lax.optimization_barrier(
-        (excess, one_row(log_ratio), live_rows)
-    )
-    mass = share(jnp.sum(excess, axis=1))
+    own = one_row(jnp.concatenate(stats_target + stats_draft))
+    stats = exchange(jnp.broadcast_to(own[None], (owners, 1, 128)), share_axes)
+    excess, mass, log_ratio = excess_of(stats, own, exp_target, exp_draft)
+    mass = exchange(mass, share_axes)
     return finish(
         excess, mass, log_ratio, live_rows, vocab_slice * owners, seq_count, draft_span
     )

time: 129 us -> 129 us (level)
  no operation moved by 1% of the time
where the time goes in v5:
time: 129 us; the launch traced here: 128 us
  blocking collectives  88.7 us (69%)
  starting transfers between devices  23.9 us (19%)
  local copies, waits for them, and re-layouts  5.78 us (4%)
  Pallas kernels  3.11 us (2%)
  waiting for transfers between devices  2.71 us (2%)
  other arithmetic  2.63 us (2%)
    all_to_all x5, blocking collectives, exchange(): return lax.all_to_all(blocks, axis, split_axis=0, concat_axis=0, tiled=True)  74.5 us
    psum x1, blocking collectives, per_device(): squares = lax.psum(jnp.sum(hidden * hidden, axis=(1, 2)), 'section')  14.2 us
    ppermute x1, starting transfers between devices, per_device(): lax.ppermute(jnp.concatenate([given, beside]), 'core', [(i, cores - 1 - i...  8.79 us
    ppermute x1, starting transfers between devices, per_device(): other = lax.ppermute(mine, 'core', [(0, 1), (1, 0)])  6.14 us
    ppermute x2, starting transfers between devices, per_device(): lax.ppermute(draft_piece(draft_block, flip), tensor_axes, [(i, i ^ flip)...  5.48 us
    all_to_all x1, starting transfers between devices, exchange(): return lax.all_to_all(blocks, axis, split_axis=0, concat_axis=0, tiled=True)  3.53 us
  transfers between devices with their start and end apart: 5, of which 2 were waited for; matrix products, arithmetic and copies ran while one was open for 3% of the time, Pallas kernels for 0%

profile of v5, /device:TPU:1, one launch (start us, length us, event | category | flops | bytes accessed | tf_op | source)
XLA Modules:
  0.0 127.8 jit_solution(8670009415876539302)
XLA Ops:
  0.7 0.8 dynamic-slice_bitcast_fusion.7
  1.4 1.1 dynamic-slice_bitcast_fusion
  2.5 8.8 %collective-permute-start = (bf16[40,4096]{1,0:T(8,128)(2,1)S(1)}, bf16[40,4096]{1,0:T(8,128)(2,1)S(1)}, u32[]{:S(2)}, u32[]{:S(2)}) collective-permute-start(bf16[40,4096]{1,0:T(8,128)(2,1)S(1)} %fusion.1), channel_id=1, source_target_pairs={{0,4},{4,0},{1,5},{5,1},{2,6},{6,2},{3,7},{7,3},{8,12},{12,8},{9,1... | collective-permute-start | bytes 983048 | tf_op jit(solution)/shard_map/ppermute | solution.py:176
  11.3 0.7 reshape.66
  12.1 0.9 dynamic-slice_convert_fusion
  13.0 0.1 multiply_convert_fusion.2
  13.1 0.8 copy.12
  13.9 3.5 %all-to-all-start = ((f16[16,2,8,512]{3,2,1,0:T(8,128)(2,1)}), f16[16,2,8,512]{3,2,1,0:T(8,128)(2,1)S(1)}, u32[]{:S(2)}, u32[]{:S(2)}) async-start(f16[16,2,8,512]{3,2,1,0:T(8,128)(2,1)} %bitcast.25), calls=%async_computation | async-start | bytes 524288 | tf_op jit(solution)/shard_map/all_to_all | solution.py:21
  17.5 3.6 %collective-permute-start.2 = (bf16[4,2048]{1,0:T(4,128)(2,1)S(1)}, bf16[4,2048]{1,0:T(4,128)(2,1)S(1)}, u32[]{:S(2)}, u32[]{:S(2)}) collective-permute-start(bf16[4,2048]{1,0:T(4,128)(2,1)S(1)} %get-tuple-element.80), channel_id=1, source_target_pairs={{0,12},{4,8},{8,4},{12,0},{16,28},{20,24},{24,20},{28,16},{32,44},... | collective-permute-start | bytes 49160 | tf_op jit(solution)/shard_map/ppermute | solution.py:193
  21.0 1.9 %collective-permute-start.1 = (bf16[4,2048]{1,0:T(4,128)(2,1)S(1)}, bf16[4,2048]{1,0:T(4,128)(2,1)S(1)}, u32[]{:S(2)}, u32[]{:S(2)}) collective-permute-start(bf16[4,2048]{1,0:T(4,128)(2,1)S(1)} %get-tuple-element.81), channel_id=1, source_target_pairs={{0,8},{4,12},{8,0},{12,4},{16,24},{20,28},{24,16},{28,20},{32,40},... | collective-permute-start | bytes 49160 | tf_op jit(solution)/shard_map/ppermute | solution.py:193
  23.0 1.7 %slice.10.top_ref = bf16[512,2048]{1,0:T(8,128)(2,1)S(1)} slice(bf16[1024,2048]{1,0:T(8,128)(2,1)} %w_hbm), slice={[0:512], [0:2048]} | slice | bytes 4194304 | tf_op jit(solution)/shard_map/slice | solution.py:198
  24.7 2.3 %all-to-all-done = f16[16,2,8,512]{3,2,1,0:T(8,128)(2,1)S(1)} async-done(((f16[16,2,8,512]{3,2,1,0:T(8,128)(2,1)}), f16[16,2,8,512]{3,2,1,0:T(8,128)(2,1)S(1)}, u32[]{:S(2)}, u32[]{:S(2)}) %all-to-all-start) | async-done | bytes 262176 | tf_op jit(solution)/shard_map/all_to_all | solution.py:21
  27.1 0.1 multiply_reduce_fusion.1
  27.2 14.2 %psum.7 = f32[2]{0:T(128)S(1)} all-reduce(f32[2]{0:T(128)S(1)} %multiply_reduce_fusion.1), channel_id=1, replica_groups=mesh['dp'=4,'zy'=16,'core'=2,'section'=4] {'section'}, use_global_device_ids=true, to_apply=%region_2.3 | all-reduce | flops 2 | bytes 16 | tf_op jit(solution)/shard_map/psum | solution.py:202
  41.6 0.1 broadcast_in_dim.15
  41.7 20.1 %all_to_all.35 = bf16[64,2,1024]{2,1,0:T(2,128)(2,1)S(1)} all-to-all(bf16[64,2,1024]{2,1,0:T(2,128)(2,1)S(1)} %bitcast.42), channel_id=1, replica_groups=mesh['dp'=4,'zy'=16,'core'=2,'section'=4] {'dp','zy'}, dimensions={0} | all-to-all | bytes 524288 | tf_op jit(solution)/shard_map/all_to_all | solution.py:21
  61.9 0.1 reshape.64
  62.0 6.1 %collective-permute-start.3 = (bf16[4,32,1024]{2,1,0:T(8,128)(2,1)S(1)}, bf16[4,32,1024]{2,1,0:T(8,128)(2,1)S(1)}, u32[]{:S(2)}, u32[]{:S(2)}) collective-permute-start(bf16[4,32,1024]{2,1,0:T(8,128)(2,1)S(1)} %reshape.64), channel_id=1, source_target_pairs={{0,4},{4,0},{1,5},{5,1},{2,6},{6,2},{3,7},{7,3},{8,12},{12,8},{9,1... | collective-permute-start | bytes 786440 | tf_op jit(solution)/shard_map/ppermute | solution.py:221
  68.2 0.2 fusion.5
  68.6 0.2 fusion.3
  68.9 0.4 collective-permute-done.3
  69.3 2.0 %head_product.1 = f32[256,2048]{1,0:T(8,128)S(1)} custom-call(bf16[256,1024]{1,0:T(8,128)(2,1)S(1)} %bitcast.38, bf16[512,2048]{1,0:T(8,128)(2,1)S(1)} %slice.10.top_ref, bf16[1024,2048]{1,0:T(8,128)(2,1)} %w_hbm), custom_call_target="tpu_custom_call" | custom-call | tf_op jit(solution)/shard_map/head_product/pallas_call | solution.py:56
  71.3 0.2 multiply_convert_fusion
  71.5 17.3 %all_to_all.36 = f16[4,64,2048]{2,1,0:T(8,128)(2,1)S(1)} all-to-all(f16[4,64,2048]{2,1,0:T(8,128)(2,1)S(1)} %bitcast.39), channel_id=1, replica_groups=mesh['dp'=4,'zy'=16,'core'=2,'section'=4] {'dp'}, dimensions={0} | all-to-all | bytes 2097152 | tf_op jit(solution)/shard_map/all_to_all | solution.py:21
  88.8 0.2 convert_reduce_fusion
  89.1 11.3 %all_to_all.37 = f16[4,16,2048]{2,1,0:T(8,128)(2,1)S(1)} all-to-all(f16[4,16,2048]{2,1,0:T(8,128)(2,1)S(1)} %bitcast.41), channel_id=1, replica_groups=mesh['dp'=4,'zy'=16,'core'=2,'section'=4] {'section'}, dimensions={0} | all-to-all | bytes 524288 | tf_op jit(solution)/shard_map/all_to_all | solution.py:21
  100.4 0.2 select_reduce_fusion
  100.6 0.2 fusion.6
  100.9 14.5 %all_to_all.38.stats_ref = f32[32,1,128]{2,1,0:T(1,128)S(1)} all-to-all(f32[32,1,128]{2,1,0:T(1,128)S(1)} %broadcast_in_dim.36), channel_id=1, replica_groups=mesh['dp'=4,'zy'=16,'core'=2,'section'=4] {'core','zy'}, dimensions={0} | all-to-all | bytes 32768 | tf_op jit(solution)/shard_map/all_to_all | solution.py:21
  115.5 0.3 excess.1
  115.8 11.2 %all_to_all.39.mass_ref = f32[32,1,128]{2,1,0:T(1,128)S(1)} all-to-all(f32[32,1,128]{2,1,0:T(1,128)S(1)} %get-tuple-element.63), channel_id=1, replica_groups=mesh['dp'=4,'zy'=16,'core'=2,'section'=4] {'core','zy'}, dimensions={0} | all-to-all | bytes 32768 | tf_op jit(solution)/shard_map/all_to_all | solution.py:21
  127.0 0.8 finish.1
  (32 shorter events, 0.8 us)
Async XLA Ops:
  0.6 16.8 %copy-start = (bf16[1,1,1,4,8192]{4,3,2,1,0:T(4,128)(2,1)S(1)}, bf16[1,1,1,4,8192]{4,3,2,1,0:T(4,128)(2,1)}, u32[]{:S(2)}) copy-start(bf16[1,1,1,4,8192]{4,3,2,1,0:T(4,128)(2,1)} %param.11) | copy-start | bytes 196612
  2.5 10.4 %collective-permute-start = (bf16[40,4096]{1,0:T(8,128)(2,1)S(1)}, bf16[40,4096]{1,0:T(8,128)(2,1)S(1)}, u32[]{:S(2)}, u32[]{:S(2)}) collective-permute-start(bf16[40,4096]{1,0:T(8,128)(2,1)S(1)} %fusion.1), channel_id=1, source_target_pairs={{0,4},{4,0},{1,5},{5,1},{2,6},{6,2},{3,7},{7,3},{8,12},{12,8},{9,1... | collective-permute-start | bytes 983048 | tf_op jit(solution)/shard_map/ppermute | solution.py:176
  13.9 13.1 %all-to-all-start = ((f16[16,2,8,512]{3,2,1,0:T(8,128)(2,1)}), f16[16,2,8,512]{3,2,1,0:T(8,128)(2,1)S(1)}, u32[]{:S(2)}, u32[]{:S(2)}) async-start(f16[16,2,8,512]{3,2,1,0:T(8,128)(2,1)} %bitcast.25), calls=%async_computation | async-start | bytes 524288 | tf_op jit(solution)/shard_map/all_to_all | solution.py:21
  17.5 9.7 %collective-permute-start.2 = (bf16[4,2048]{1,0:T(4,128)(2,1)S(1)}, bf16[4,2048]{1,0:T(4,128)(2,1)S(1)}, u32[]{:S(2)}, u32[]{:S(2)}) collective-permute-start(bf16[4,2048]{1,0:T(4,128)(2,1)S(1)} %get-tuple-element.80), channel_id=1, source_target_pairs={{0,12},{4,8},{8,4},{12,0},{16,28},{20,24},{24,20},{28,16},{32,44},... | collective-permute-start | bytes 49160 | tf_op jit(solution)/shard_map/ppermute | solution.py:193
  21.0 6.2 %collective-permute-start.1 = (bf16[4,2048]{1,0:T(4,128)(2,1)S(1)}, bf16[4,2048]{1,0:T(4,128)(2,1)S(1)}, u32[]{:S(2)}, u32[]{:S(2)}) collective-permute-start(bf16[4,2048]{1,0:T(4,128)(2,1)S(1)} %get-tuple-element.81), channel_id=1, source_target_pairs={{0,8},{4,12},{8,0},{12,4},{16,24},{20,28},{24,16},{28,20},{32,40},... | collective-permute-start | bytes 49160 | tf_op jit(solution)/shard_map/ppermute | solution.py:193
  24.7 43.5 %copy-start.1 = (s32[4,4]{1,0:T(4,128)S(1)}, s32[4,4]{1,0:T(4,128)}, u32[]{:S(2)}) copy-start(s32[4,4]{1,0:T(4,128)} %param.12) | copy-start | bytes 196
  24.7 43.8 %copy-start.2 = (s32[4]{0:T(128)S(1)}, s32[4]{0:T(128)}, u32[]{:S(2)}) copy-start(s32[4]{0:T(128)} %param.13) | copy-start | bytes 52
  62.0 7.3 %collective-permute-start.3 = (bf16[4,32,1024]{2,1,0:T(8,128)(2,1)S(1)}, bf16[4,32,1024]{2,1,0:T(8,128)(2,1)S(1)}, u32[]{:S(2)}, u32[]{:S(2)}) collective-permute-start(bf16[4,32,1024]{2,1,0:T(8,128)(2,1)S(1)} %reshape.64), channel_id=1, source_target_pairs={{0,4},{4,0},{1,5},{5,1},{2,6},{6,2},{3,7},{7,3},{8,12},{12,8},{9,1... | collective-permute-start | bytes 786440 | tf_op jit(solution)/shard_map/ppermute | solution.py:221
